TPU v7x, 256 devices: a whole 4x4x8 slice. The times are simulated.
256 devices in a mesh: rep: 64 (over x, y, z_hi, core), fsdp: 4 (over z_lo).
Axes of the slice: x: 4, y: 4, z: 8 (z_hi: 2, z_lo: 4; z = z_hi * 4 + z_lo), core: 2. Of those that a mesh axis runs over, the one named last changes fastest.
Arguments:
- activations: bfloat16 [65536, 8192], P(('rep', 'fsdp')), may hold values from -6 to 6
- norm_gain: bfloat16 [64, 8192], P('rep', 'fsdp'), may hold values from 0.5 to 1.5
- key_weight: bfloat16 [64, 8192, 512], P('rep', 'fsdp'), may hold values from -6 to 6
- key_cotangent: bfloat16 [65536, 512], P(('rep', 'fsdp')), may hold values from -6 to 6
- outer_params: float32 [8192, 128], P('fsdp'), may hold values from -6 to 6
- outer_momentum: float32 [8192, 128], P('fsdp'), may hold values from -3 to 3
- fragment: int32 [1], replicated, may hold values from 0 to 1048575
Outputs:
- keys: bfloat16 [65536, 512], P(('rep', 'fsdp'))
- input_grad: bfloat16 [65536, 8192], P(('rep', 'fsdp'))
- weight_grad: bfloat16 [64, 8192, 512], P('rep', 'fsdp')
- gain_grad: float32 [64, 8192], P('rep', 'fsdp')
- new_params: float32 [8192, 128], P('fsdp')
- new_momentum: float32 [8192, 128], P('fsdp')
All inputs are finite; a program needn't handle non-finite values.
Results may differ from a plain program's by a relative error of at most 0.015.
Values may be sent and summed in bfloat16 or wider, within the bound.
No kernel may reach another device: no remote copies, remote signals or barrier semaphores. Data moves between devices by JAX's collectives and lax.ppermute only.
A program may use at most 128 MiB of HBM per device.

v0:
```python
import jax
import jax.numpy as jnp
from jax import lax
from jax.sharding import PartitionSpec as P

outer_rate = 0.7
momentum_decay = 0.9
epsilon = 1e-05


def nesterov(params, moment, increment):
    moment_next = momentum_decay * moment + increment
    return (params - outer_rate * (increment + momentum_decay * moment_next), moment_next)


def body(activations, norm_gain, key_weight, key_cotangent, outer_params, outer_momentum, fragment):
    model_width = activations.shape[1]
    head_size = outer_params.shape[1]
    key_width = key_cotangent.shape[1]
    factor = model_width ** (-0.5)
    replicas = lax.axis_size("rep")
    column_start = fragment[0] % (key_width // head_size) * head_size
    local_block = lax.dynamic_slice_in_dim(key_weight[0], column_start, head_size, 1).astype(
        jnp.float32
    )
    pseudo_term = outer_params - local_block
    summed_delta = lax.psum(pseudo_term, "rep")
    new_params, new_momentum = nesterov(outer_params, outer_momentum, summed_delta / replicas)
    transposed = (((1,), (1,)), ((), ()))
    contract_tokens = (((0,), (0,)), ((), ()))
    xfloat = activations.astype(jnp.float32)
    inverse = lax.rsqrt(jnp.mean(xfloat * xfloat, axis=1, keepdims=True) + epsilon)
    normed = xfloat * inverse
    gain_piece = lax.all_gather(norm_gain, "fsdp", axis=1, tiled=True)
    weight_block = lax.all_gather(key_weight, "fsdp", axis=1, tiled=True)
    gain_float = gain_piece[0].astype(jnp.float32)
    scaled = (normed * gain_float).astype(jnp.bfloat16)
    running = jnp.dot(scaled, weight_block[0], preferred_element_type=jnp.float32)
    upstream = (
        lax.dot_general(
            key_cotangent,
            lax.all_gather(key_weight, "fsdp", axis=1, tiled=True)[0],
            transposed,
            preferred_element_type=jnp.float32,
        )
        * factor
    )
    keys = (running * factor).astype(jnp.bfloat16)
    adjusted = upstream * gain_float
    project = jnp.mean(adjusted * normed, axis=1, keepdims=True)
    input_grad = (inverse * (adjusted - normed * project)).astype(jnp.bfloat16)
    gain_term = jnp.sum(upstream * normed, axis=0)
    gain_grad = lax.psum_scatter(
        gain_term.astype(jnp.bfloat16), "fsdp", scatter_dimension=0, tiled=True
    ).astype(jnp.float32)[None, :]
    partial_value = (
        lax.dot_general(scaled, key_cotangent, contract_tokens, preferred_element_type=jnp.float32)
        * factor
    )
    summed = lax.psum_scatter(
        lax.optimization_barrier(partial_value.astype(jnp.bfloat16))
        .astype(jnp.float32)
        .astype(jnp.bfloat16),
        "fsdp",
        scatter_dimension=0,
        tiled=True,
    )
    weight_grad = summed[None]
    return (keys, input_grad, weight_grad, gain_grad, new_params, new_momentum)


def solution(mesh):
    in_specs = (
        P(("rep", "fsdp"), None),
        P("rep", "fsdp"),
        P("rep", "fsdp", None),
        P(("rep", "fsdp"), None),
        P("fsdp", None),
        P("fsdp", None),
        P(),
    )
    out_specs = (
        P(("rep", "fsdp"), None),
        P(("rep", "fsdp"), None),
        P("rep", "fsdp", None),
        P("rep", "fsdp"),
        P("fsdp", None),
        P("fsdp", None),
    )
    return jax.shard_map(body, mesh=mesh, in_specs=in_specs, out_specs=out_specs, check_vma=False)
```

profile of v0, /device:TPU:1, one launch (start us, length us, event | category | flops | bytes accessed | tf_op | source)
XLA Modules:
  0.0 1075.9 jit_solution(3346609719145150579)
XLA Ops:
  8.0 0.0 copy-start
  8.0 0.0 all-reduce.3.cloned.1.call-start
  8.8 2.4 convert_subtract_fusion
  11.2 0.0 all-reduce.3.cloned.1.call-update
  11.2 0.0 all-gather.2.cloned.1.call-start
  11.3 0.5 all-gather.2.cloned.1.call-update
  11.8 0.0 reduce-scatter.2.cloned.1.call-start
  11.8 12.7 %all_gather.7 = bf16[1,8192]{1,0:T(2,128)(2,1)S(1)} all-gather(bf16[1,2048]{1,0:T(2,128)(2,1)} %param.8), channel_id=1, replica_groups=mesh['rep'=64,'fsdp'=4] {'fsdp'}, dimensions={1}, use_global_device_ids=true | all-gather | bytes 20480 | tf_op jit(solution)/shard_map/all_gather | solution.py:34
  24.6 3.1 fusion.10
  27.7 0.0 copy-done
  27.7 8.8 multiply_convert_fusion
  36.5 0.0 reduce-scatter.2.cloned.1.call-update
  36.5 0.6 copy-done.5
  37.2 0.6 dynamic-slice.1
  38.4 990.4 %all-reduce.3.cloned.1.call-done = f32[2048,128]{1,0:T(8,128)} async-done(((f32[2048,128]{1,0:T(8,128)}), f32[2048,128]{1,0:T(8,128)}) %all-reduce.3.cloned.1.call-update) | async-done | bytes 1048592 | tf_op jit(solution)/shard_map/psum | solution.py:27
  1028.8 0.0 copy-done.3
  1028.8 0.0 copy-done.4
  1028.8 2.9 multiply_subtract_fusion
  1031.7 11.9 %fusion.9 = (bf16[8192]{0:T(1024)(128)(2,1)S(1)}, f32[256]{0:T(256)S(1)}, f32[256,8192]{1,0:T(8,128)}) fusion(bf16[256,8192]{1,0:T(8,128)(2,1)} %param.7, f32[256]{0:T(256)S(1)} %add_rsqrt_fusion, f32[8192]{0:T(1024)S(1)} %broadcast_multiply_fusion, bf16[256,512]{1,0:T(8,128)(2,1)S(1)} %copy-done, bf16[1,8192,512]{2,1,0:T(8,128)(2,1)} %all-gather.2.cloned.1.call-done), kind=kOutput, calls=%fused_computation.12 | convolution fusion | flops 2164252416 | bytes 21284864 | tf_op jit(solution)/shard_map/dot_general | solution.py:40
  1043.7 12.4 %all-reduce = bf16[8192]{0:T(1024)(128)(2,1)S(1)} all-reduce(bf16[8192]{0:T(1024)(128)(2,1)S(1)} %get-tuple-element.6), channel_id=3, replica_groups=mesh['rep'=64,'fsdp'=4] {'fsdp'}, use_global_device_ids=true, to_apply=%region_4.5.clone | all-reduce | flops 8192 | bytes 32768
  1056.1 0.6 dynamic-slice_convert_fusion
  1056.7 7.9 fusion.18
  1064.6 0.5 copy-done.2
  1065.1 3.4 fusion.8
  (12 shorter events, 0.1 us)
Async XLA Ops:
  8.0 19.7 %copy-start = (bf16[256,512]{1,0:T(8,128)(2,1)S(1)}, bf16[256,512]{1,0:T(8,128)(2,1)}, u32[]{:S(2)}) copy-start(bf16[256,512]{1,0:T(8,128)(2,1)} %param.10) | copy-start | bytes 786436
  8.0 1020.8 %all-reduce.3.cloned.1.call-start = ((), (), s32[]{:S(2)}) async-start(), calls=%async_computation.3 | async-start | bytes 2097152 | tf_op jit(solution)/shard_map/psum | solution.py:27
  11.2 1020.5 %all-gather.2.cloned.1.call-start = ((), (), s32[]{:S(2)}) async-start(), calls=%async_computation.1 | async-start | bytes 10485760 | tf_op jit(solution)/shard_map/all_gather | solution.py:35
  11.8 1056.7 %reduce-scatter.2.cloned.1.call-start = ((), (), s32[]{:S(2)}) async-start(), calls=%async_computation.2 | async-start | bytes 10485760 | tf_op jit(solution)/shard_map/reduce_scatter | solution.py:60
  36.5 0.7 copy-start.5
  36.5 992.3 %copy-start.3 = (f32[2048,128]{1,0:T(8,128)S(1)}, f32[2048,128]{1,0:T(8,128)}, u32[]{:S(2)}) copy-start(f32[2048,128]{1,0:T(8,128)} %param.11) | copy-start | bytes 3145732
  36.5 992.3 %copy-start.4 = (f32[2048,128]{1,0:T(8,128)S(1)}, f32[2048,128]{1,0:T(8,128)}, u32[]{:S(2)}) copy-start(f32[2048,128]{1,0:T(8,128)} %param.12) | copy-start | bytes 3145732
  1056.7 7.9 copy-start.1
  1056.7 8.4 copy-start.2
Sparse Core Ops, SparseCore 0:
  12.0 1016.6 all-reduce.2
Sparse Core Ops, SparseCore 1:
  13.5 157.6 all-gather.1
  174.1 151.3 reduce-scatter.1
where the time goes:
time: 1080 us
  waiting for transfers between devices  991 us (92%)
  matrix products  28.6 us (3%)
  blocking collectives  25.1 us (2%)
  between operations  16.9 us (2%)
  other arithmetic  12.5 us (1%)
    psum x1, waiting for transfers between devices, body(): summed_delta = lax.psum(pseudo_term, 'rep')  990 us
  transfers between devices with their start and end apart: 3, of which 1 were waited for; matrix products, arithmetic and copies ran while one was open for 4% of the time, Pallas kernels for 0%

commit v1 on v0

v1 whole, which is shorter than its diff:
```python
import jax
import jax.numpy as jnp
from jax import lax
from jax.sharding import Mesh, PartitionSpec as P

outer_rate = 0.7
momentum_decay = 0.9
epsilon = 1e-05

PIECES = 2
RIGHT = [(0, 1), (1, 2), (2, 3)]
LEFT = [(1, 0), (2, 1), (3, 2)]
CONTRACT_ROWS = (((0,), (0,)), ((), ()))
CONTRACT_COLUMNS = (((1,), (1,)), ((), ()))
f32, bf16 = jnp.float32, jnp.bfloat16


def dot(a, b, dims=(((1,), (0,)), ((), ()))):
    return lax.dot_general(a, b, dims, preferred_element_type=f32)


def swap(value, axis):
    return lax.ppermute(value, axis, [(0, 1), (1, 0)])


def shifts(size):
    return sorted(range(1, size), key=lambda k: -min(k, size - k) == -size // 2)


def scatter_sum(value, axis, size):
    me = lax.axis_index(axis)
    rows = value.shape[0] // size
    total = lax.dynamic_slice_in_dim(value, me * rows, rows, 0)
    parts = []
    for k in range(1, size):
        block = lax.dynamic_slice_in_dim(value, (me + k) % size * rows, rows, 0)
        parts.append(lax.ppermute(block, axis, [(j, (j + k) % size) for j in range(size)]))
    for part in parts:
        total = total + part
    return total


def gather_rows(value, axis, size):
    me = lax.axis_index(axis)
    rows = value.shape[0]
    parts = [value] + [
        lax.ppermute(value, axis, [(j, (j + k) % size) for j in range(size)])
        for k in range(1, size)
    ]
    whole = jnp.zeros((rows * size,) + value.shape[1:], value.dtype)
    for k, part in enumerate(parts):
        whole = lax.dynamic_update_slice_in_dim(whole, part, (me - k + size) % size * rows, 0)
    return whole


def replica_sum(term, sizes):
    total = scatter_sum(term, "core", sizes["core"])
    total = scatter_sum(total, "x", sizes["x"])
    total = scatter_sum(total, "y", sizes["y"])
    total = total + swap(total, "zh")
    total = gather_rows(total, "y", sizes["y"])
    total = gather_rows(total, "x", sizes["x"])
    return gather_rows(total, "core", sizes["core"])


def body(sizes, activations, norm_gain, key_weight, key_cotangent, outer_params, outer_momentum, fragment):
    n = sizes["fsdp"]
    tokens, model_width = activations.shape
    key_width = key_cotangent.shape[1]
    head_size = outer_params.shape[1]
    shard = key_weight.shape[1]
    rows = shard // PIECES
    factor = model_width ** (-0.5)
    me = lax.axis_index("fsdp")
    weight = key_weight[0]
    gain = norm_gain[0].astype(f32)[:, None]

    scaled = (weight.astype(f32) * gain).astype(bf16)
    to_right = [scaled[c * rows : (c + 1) * rows] for c in range(PIECES)]
    to_left = to_right
    got_right, got_left = [], []
    for c in range(PIECES):
        got_right.append(lax.ppermute(to_right[c], "fsdp", RIGHT))
        got_left.append(lax.ppermute(to_left[c], "fsdp", LEFT))

    xfloat = activations.astype(f32)
    inverse = lax.rsqrt(jnp.mean(xfloat * xfloat, axis=1, keepdims=True) + epsilon)
    cotangent = (key_cotangent.astype(f32) * inverse).astype(bf16)

    def own_partial(owner, c):
        start = jnp.clip(owner, 0, n - 1) * shard + c * rows
        columns = lax.dynamic_slice_in_dim(activations, start, rows, 1)
        return dot(columns, cotangent, CONTRACT_ROWS)

    arrived_right, arrived_left = [got_right], [got_left]
    for s in range(1, n):
        next_right, next_left = [], []
        for c in range(PIECES):
            part = jnp.where(me < s, own_partial(n - s + me, c), 0.0)
            out = (got_right[c].astype(f32) + part).astype(bf16)
            next_right.append(lax.ppermute(out, "fsdp", RIGHT))
            part = jnp.where(me > n - 1 - s, own_partial(me + s - n, c), 0.0)
            out = (got_left[c].astype(f32) + part).astype(bf16)
            next_left.append(lax.ppermute(out, "fsdp", LEFT))
        got_right, got_left = next_right, next_left
        if s < n - 1:
            arrived_right.append(got_right)
            arrived_left.append(got_left)

    whole = jnp.zeros((model_width, key_width), bf16)
    whole = lax.dynamic_update_slice_in_dim(whole, scaled, me * shard, 0)
    for o in range(1, n):
        for c in range(PIECES):
            piece = jnp.where(me >= o, arrived_right[o - 1][c], arrived_left[n - 1 - o][c])
            whole = lax.dynamic_update_slice_in_dim(whole, piece, (me - o + n) % n * shard + c * rows, 0)

    keys_float = dot(activations, whole) * (inverse * factor)
    keys = keys_float.astype(bf16)
    project = jnp.sum(keys_float * key_cotangent.astype(f32), axis=1, keepdims=True) / model_width
    adjusted = dot(key_cotangent, whole, CONTRACT_COLUMNS) * factor
    input_grad = (inverse * (adjusted - xfloat * (inverse * project))).astype(bf16)

    weight_grad, gain_grad = [], []
    for c in range(PIECES):
        summed = (got_right[c].astype(f32) + got_left[c].astype(f32) + own_partial(me, c)) * factor
        part = slice(c * rows, (c + 1) * rows)
        weight_grad.append((summed * gain[part]).astype(bf16))
        gain_grad.append(jnp.sum(summed * weight[part].astype(f32), axis=1))
    weight_grad = jnp.concatenate(weight_grad, 0)[None]
    gain_grad = jnp.concatenate(gain_grad, 0)[None]

    column_start = fragment[0] % (key_width // head_size) * head_size
    local_block = lax.dynamic_slice_in_dim(weight, column_start, head_size, 1).astype(f32)
    replicas = sizes["x"] * sizes["y"] * sizes["zh"] * sizes["core"]
    increment = replica_sum(outer_params - local_block, sizes) / replicas
    new_momentum = momentum_decay * outer_momentum + increment
    new_params = outer_params - outer_rate * (increment + momentum_decay * new_momentum)
    return (keys, input_grad, weight_grad, gain_grad, new_params, new_momentum)


def solution(mesh):
    sizes = {"x": 4, "y": 4, "zh": 2, "core": 2, "fsdp": 4}
    fine = Mesh(mesh.devices.reshape(tuple(sizes.values())), tuple(sizes))
    rep = ("x", "y", "zh", "core")
    both = rep + ("fsdp",)
    in_specs = (
        P(both, None),
        P(rep, "fsdp"),
        P(rep, "fsdp", None),
        P(both, None),
        P("fsdp", None),
        P("fsdp", None),
        P(),
    )
    out_specs = (
        P(both, None),
        P(both, None),
        P(rep, "fsdp", None),
        P(rep, "fsdp"),
        P("fsdp", None),
        P("fsdp", None),
    )

    def local(*args):
        return body(sizes, *args)

    return jax.shard_map(local, mesh=fine, in_specs=in_specs, out_specs=out_specs, check_vma=False)
```

time: 1080 us -> 282 us (0.26)
  waiting for transfers between devices: 991 us -> 96.7 us
  starting transfers between devices: 0.12 us -> 89.8 us
  blocking collectives: 25.1 us -> 0 us
  local copies, waits for them, and re-layouts: 1.76 us -> 24.1 us
  other arithmetic: 12.5 us -> 28.5 us
  between operations: 16.9 us -> 2.07 us
    psum x1 -> x0, waiting for transfers between devices: 990 us -> none  [body(): summed_delta = lax.psum(pseudo_term, 'rep')]
    ppermute x0 -> x31, waiting for transfers between devices: none -> 96.7 us  [the longest x6 77.8 us: body(): next_left.append(lax.ppermute(out, 'fsdp', LEFT))]
    ppermute x0 -> x31, starting transfers between devices: none -> 89.8 us  [the longest x6 26.6 us: body(): next_right.append(lax.ppermute(out, 'fsdp', RIGHT))]
    unnamed x13 -> x50, local copies, waits for them, and re-layouts: 1.76 us -> 16.1 us
    all_gather x1 -> x0, blocking collectives: 12.7 us -> none  [body(): gain_piece = lax.all_gather(norm_gain, 'fsdp', axis=1, tiled=True)]
    unnamed x1 -> x0, blocking collectives: 12.4 us -> none
    dynamic_update_slice x0 -> x8, other arithmetic: none -> 12 us  [the longest x6 9.44 us: body(): lax.dynamic_update_slice_in_dim(whole, piece, (me - o + n) % n * shard +...]
    dot_general x3 -> x16, matrix products: 28.6 us -> 37.1 us  [dot(): return lax.dot_general(a, b, dims, preferred_element_type=f32)]
  transfers between devices with their start and end apart: 3 -> 31, of which waited for: 1 -> 15; matrix products, arithmetic and copies ran while one was open for 4% -> 24% of each run, Pallas kernels for 0% -> 0%
where the time goes in v1:
time: 282 us; the launch traced here: 278 us
  waiting for transfers between devices  96.7 us (34%)
  starting transfers between devices  89.8 us (32%)
  matrix products  37.1 us (13%)
  other arithmetic  28.5 us (10%)
  local copies, waits for them, and re-layouts  24.1 us (9%)
    ppermute x6, waiting for transfers between devices, body(): next_left.append(lax.ppermute(out, 'fsdp', LEFT))  77.8 us
    dot_general x16, matrix products, dot(): return lax.dot_general(a, b, dims, preferred_element_type=f32)  37.1 us
    ppermute x6, starting transfers between devices, body(): next_right.append(lax.ppermute(out, 'fsdp', RIGHT))  26.6 us
    ppermute x2, starting transfers between devices, body(): got_right.append(lax.ppermute(to_right[c], 'fsdp', RIGHT))  25.6 us
    unnamed x50, local copies, waits for them, and re-layouts  16.1 us
    ppermute x7, starting transfers between devices, scatter_sum(): lax.ppermute(block, axis, [(j, (j + k) % size) for j in range(size)])  10.7 us
    ppermute x7, starting transfers between devices, gather_rows(): lax.ppermute(value, axis, [(j, (j + k) % size) for j in range(size)])  10.3 us
    dynamic_update_slice x6, other arithmetic, body(): lax.dynamic_update_slice_in_dim(whole, piece, (me - o + n) % n * shard +...  9.44 us
  transfers between devices with their start and end apart: 31, of which 15 were waited for; matrix products, arithmetic and copies ran while one was open for 24% of the time, Pallas kernels for 0%

profile of v1, /device:TPU:1, one launch (start us, length us, event | category | flops | bytes accessed | tf_op | source)
XLA Modules:
  0.0 278.2 jit_solution(2350057209647670379)
XLA Ops:
  6.9 3.8 %broadcast_in_dim.36 = bf16[8192,512]{1,0:T(8,128)(2,1)} broadcast(bf16[]{:T(256)} %constant.175.clone.1), dimensions={} | broadcast | bytes 8388610 | tf_op jit(solution)/shard_map/broadcast_in_dim | solution.py:110
  18.1 6.4 %copy.14 = bf16[256,8192]{0,1:T(8,128)(2,1)} copy(bf16[256,8192]{1,0:T(8,128)(2,1)} %param.7) | data formatting | bytes 8388608 | tf_op args[0]
  30.1 3.3 %fusion.4 = f32[256]{0:T(256)S(1)} fusion(bf16[256,8192]{0,1:T(8,128)(2,1)} %copy.14), kind=kLoop, calls=%fused_computation.7 | loop fusion | flops 6291200 | bytes 4195328 | tf_op jit(solution)/shard_map/reduce_sum | solution.py:87
  34.9 3.7 %collective-permute-done.17 = f32[256,128]{1,0:T(8,128)S(1)} collective-permute-done((f32[256,128]{1,0:T(8,128)S(1)}, f32[256,128]{1,0:T(8,128)S(1)}, u32[]{:S(2)}, u32[]{:S(2)}) %collective-permute-start.17) | collective-permute-done | bytes 131104 | tf_op jit(solution)/shard_map/ppermute | solution.py:37
  49.3 6.0 %collective-permute-start.23 = (f32[64,128]{1,0:T(8,128)}, f32[64,128]{1,0:T(8,128)}, u32[]{:S(2)}, u32[]{:S(2)}) collective-permute-start(f32[64,128]{1,0:T(8,128)} %add_add_fusion.3), channel_id=1, source_target_pairs={{0,8},{8,0},{1,9},{9,1},{2,10},{10,2},{3,11},{11,3},{4,12},{12,4},... | collective-permute-start | bytes 98312 | tf_op jit(solution)/shard_map/ppermute | solution.py:23
  68.0 5.6 %collective-permute-done.27 = f32[256,128]{1,0:T(8,128)} collective-permute-done((f32[256,128]{1,0:T(8,128)S(1)}, f32[256,128]{1,0:T(8,128)}, u32[]{:S(2)}, u32[]{:S(2)}) %collective-permute-start.27) | collective-permute-done | bytes 131104 | tf_op jit(solution)/shard_map/ppermute | solution.py:47
  74.5 22.8 %collective-permute-start.4 = (bf16[1024,512]{1,0:T(8,128)(2,1)}, bf16[1024,512]{1,0:T(8,128)(2,1)S(1)}, u32[]{:S(2)}, u32[]{:S(2)}) collective-permute-start(bf16[1024,512]{1,0:T(8,128)(2,1)} %get-tuple-element.22), channel_id=1, source_target_pairs={{0,1},{1,2},{2,3},{4,5},{5,6},{6,7},{8,9},{9,10},{10,11},{12,13},{... | collective-permute-start | bytes 3145736 | tf_op jit(solution)/shard_map/ppermute | solution.py:83
  97.4 5.9 %collective-permute-start.30 = (f32[1024,128]{1,0:T(8,128)S(1)}, f32[1024,128]{1,0:T(8,128)S(1)}, u32[]{:S(2)}, u32[]{:S(2)}) collective-permute-start(f32[1024,128]{1,0:T(8,128)S(1)} %constant_dynamic-update-slice_fusion.2), channel_id=1, source_target_pairs={{0,4},{4,0},{1,5},{5,1},{2,6},{6,2},{3,7},{7,3},{8,12},{12,8},{9,1... | collective-permute-start | bytes 1572872 | tf_op jit(solution)/shard_map/ppermute | solution.py:47
  110.2 5.0 %collective-permute-start.8 = (bf16[1024,512]{1,0:T(8,128)(2,1)S(1)}, bf16[1024,512]{1,0:T(8,128)(2,1)S(1)}, u32[]{:S(2)}, u32[]{:S(2)}) collective-permute-start(bf16[1024,512]{1,0:T(8,128)(2,1)S(1)} %add_convert_fusion.7), channel_id=1, source_target_pairs={{0,1},{1,2},{2,3},{4,5},{5,6},{6,7},{8,9},{9,10},{10,11},{12,13},{... | collective-permute-start | bytes 3145736 | tf_op jit(solution)/shard_map/ppermute | solution.py:101
  115.7 3.4 %collective-permute-start.9 = (bf16[1024,512]{1,0:T(8,128)(2,1)S(1)}, bf16[1024,512]{1,0:T(8,128)(2,1)S(1)}, u32[]{:S(2)}, u32[]{:S(2)}) collective-permute-start(bf16[1024,512]{1,0:T(8,128)(2,1)S(1)} %add_convert_fusion.6), channel_id=1, source_target_pairs={{0,1},{1,2},{2,3},{4,5},{5,6},{6,7},{8,9},{9,10},{10,11},{12,13},{... | collective-permute-start | bytes 3145736 | tf_op jit(solution)/shard_map/ppermute | solution.py:101
  119.1 13.2 %collective-permute-done.2 = bf16[1024,512]{1,0:T(8,128)(2,1)S(1)} collective-permute-done((bf16[1024,512]{1,0:T(8,128)(2,1)S(1)}, bf16[1024,512]{1,0:T(8,128)(2,1)S(1)}, u32[]{:S(2)}, u32[]{:S(2)}) %collective-permute-start.2) | collective-permute-done | bytes 1048608 | tf_op jit(solution)/shard_map/ppermute | solution.py:104
  134.3 20.5 %collective-permute-done.6 = bf16[1024,512]{1,0:T(8,128)(2,1)S(1)} collective-permute-done((bf16[1024,512]{1,0:T(8,128)(2,1)S(1)}, bf16[1024,512]{1,0:T(8,128)(2,1)S(1)}, u32[]{:S(2)}, u32[]{:S(2)}) %collective-permute-start.6) | collective-permute-done | bytes 1048608 | tf_op jit(solution)/shard_map/ppermute | solution.py:104
  158.7 4.1 %collective-permute-start.10 = (bf16[1024,512]{1,0:T(8,128)(2,1)S(1)}, bf16[1024,512]{1,0:T(8,128)(2,1)S(1)}, u32[]{:S(2)}, u32[]{:S(2)}) collective-permute-start(bf16[1024,512]{1,0:T(8,128)(2,1)S(1)} %add_convert_fusion.5), channel_id=1, source_target_pairs={{0,1},{1,2},{2,3},{4,5},{5,6},{6,7},{8,9},{9,10},{10,11},{12,13},{... | collective-permute-start | bytes 3145736 | tf_op jit(solution)/shard_map/ppermute | solution.py:101
  163.3 3.4 %collective-permute-start.11 = (bf16[1024,512]{1,0:T(8,128)(2,1)S(1)}, bf16[1024,512]{1,0:T(8,128)(2,1)S(1)}, u32[]{:S(2)}, u32[]{:S(2)}) collective-permute-start(bf16[1024,512]{1,0:T(8,128)(2,1)S(1)} %add_convert_fusion.4), channel_id=1, source_target_pairs={{0,1},{1,2},{2,3},{4,5},{5,6},{6,7},{8,9},{9,10},{10,11},{12,13},{... | collective-permute-start | bytes 3145736 | tf_op jit(solution)/shard_map/ppermute | solution.py:101
  166.7 10.6 %collective-permute-done.3 = bf16[1024,512]{1,0:T(8,128)(2,1)S(1)} collective-permute-done((bf16[1024,512]{1,0:T(8,128)(2,1)S(1)}, bf16[1024,512]{1,0:T(8,128)(2,1)S(1)}, u32[]{:S(2)}, u32[]{:S(2)}) %collective-permute-start.3) | collective-permute-done | bytes 1048608 | tf_op jit(solution)/shard_map/ppermute | solution.py:104
  178.6 21.1 %collective-permute-done.7 = bf16[1024,512]{1,0:T(8,128)(2,1)S(1)} collective-permute-done((bf16[1024,512]{1,0:T(8,128)(2,1)S(1)}, bf16[1024,512]{1,0:T(8,128)(2,1)S(1)}, u32[]{:S(2)}, u32[]{:S(2)}) %collective-permute-start.7) | collective-permute-done | bytes 1048608 | tf_op jit(solution)/shard_map/ppermute | solution.py:104
  209.5 6.6 %fusion.10 = (f32[256]{0:T(256)S(1)}, bf16[256,512]{0,1:T(8,128)(2,1)}) fusion(bf16[256,512]{0,1:T(8,128)(2,1)S(1)} %copy.13, f32[256]{0:T(256)S(1)} %copy-done.22, bf16[8192,512]{1,0:T(8,128)(2,1)} %select_dynamic-update-slice_fusion, bf16[256,8192]{1,0:T(8,128)(2,1)S(1)} %copy-done.2), kind=kOutput, calls=%fused_computation.45 | convolution fusion | flops 2148138752 | bytes 13109248 | tf_op jit(solution)/shard_map/dot_general | solution.py:19
  224.5 5.9 %collective-permute-start.12 = (bf16[1024,512]{1,0:T(8,128)(2,1)}, bf16[1024,512]{1,0:T(8,128)(2,1)}, u32[]{:S(2)}, u32[]{:S(2)}) collective-permute-start(bf16[1024,512]{1,0:T(8,128)(2,1)} %add_convert_fusion.3), channel_id=1, source_target_pairs={{0,1},{1,2},{2,3},{4,5},{5,6},{6,7},{8,9},{9,10},{10,11},{12,13},{... | collective-permute-start | bytes 3145736 | tf_op jit(solution)/shard_map/ppermute | solution.py:101
  237.0 5.0 %collective-permute-start.14 = (bf16[1024,512]{1,0:T(8,128)(2,1)}, bf16[1024,512]{1,0:T(8,128)(2,1)}, u32[]{:S(2)}, u32[]{:S(2)}) collective-permute-start(bf16[1024,512]{1,0:T(8,128)(2,1)} %add_convert_fusion.1), channel_id=1, source_target_pairs={{0,1},{1,2},{2,3},{4,5},{5,6},{6,7},{8,9},{9,10},{10,11},{12,13},{... | collective-permute-start | bytes 3145736 | tf_op jit(solution)/shard_map/ppermute | solution.py:101
  242.0 7.9 %fusion.3 = bf16[256,8192]{0,1:T(8,128)(2,1)} fusion(bf16[8192,512]{1,0:T(8,128)(2,1)} %select_dynamic-update-slice_fusion, bf16[256,512]{1,0:T(8,128)(2,1)S(1)} %copy-done.15, bf16[256,8192]{0,1:T(8,128)(2,1)S(1)} %copy-done, f32[256]{0:T(256)S(1)} %multiply_multiply_fusion, f32[256]{0:T(256)S(1)} %copy-done.18), kind=kOutput, calls=%fused_computation.6 | convolution fusion | flops 2160066560 | bytes 17041408 | tf_op jit(solution)/shard_map/dot_general | solution.py:19
  249.9 6.3 %copy.16 = bf16[256,8192]{1,0:T(8,128)(2,1)} copy(bf16[256,8192]{0,1:T(8,128)(2,1)} %fusion.3) | data formatting | bytes 8388608
  256.2 12.3 %collective-permute-done.15 = bf16[1024,512]{1,0:T(8,128)(2,1)} collective-permute-done((bf16[1024,512]{1,0:T(8,128)(2,1)}, bf16[1024,512]{1,0:T(8,128)(2,1)}, u32[]{:S(2)}, u32[]{:S(2)}) %collective-permute-start.15) | collective-permute-done | bytes 1048608 | tf_op jit(solution)/shard_map/ppermute | solution.py:104
  268.5 3.6 %collective-permute-done.14 = bf16[1024,512]{1,0:T(8,128)(2,1)} collective-permute-done((bf16[1024,512]{1,0:T(8,128)(2,1)}, bf16[1024,512]{1,0:T(8,128)(2,1)}, u32[]{:S(2)}, u32[]{:S(2)}) %collective-permute-start.14) | collective-permute-done | bytes 1048608 | tf_op jit(solution)/shard_map/ppermute | solution.py:101
  272.1 4.0 %fusion.7 = (f32[1024]{0:T(1024)S(1)}, f32[1024]{0:T(1024)S(1)}, bf16[1024,512]{1,0:T(8,128)(2,1)S(1)}, bf16[1024,512]{1,0:T(8,128)(2,1)S(1)}) fusion(bf16[1,2048,512]{2,1,0:T(8,128)(2,1)S(1)} %copy-done.1, f32[1024,512]{1,0:T(8,128)} %fusion.15, bf16[1024,512]{1,0:T(8,128)(2,1)S(1)} %collective-permute-done.13, ...), kind=kLoop, calls=%fused_computation.14 | loop fusion | flops 10483712 | bytes 12599296 | tf_op jit(solution)/shard_map/reduce_sum | solution.py:128
  (142 shorter events, 85.8 us)
Async XLA Ops:
  3.6 20.8 %collective-permute-start.16 = (f32[1024,128]{1,0:T(8,128)}, f32[1024,128]{1,0:T(8,128)}, u32[]{:S(2)}, u32[]{:S(2)}) collective-permute-start(f32[1024,128]{1,0:T(8,128)} %constant_dynamic-slice_fusion.6), channel_id=1, source_target_pairs={{0,4},{4,0},{1,5},{5,1},{2,6},{6,2},{3,7},{7,3},{8,12},{12,8},{9,1... | collective-permute-start | bytes 1572872 | tf_op jit(solution)/shard_map/ppermute | solution.py:37
  14.0 94.5 %collective-permute-start = (bf16[1024,512]{1,0:T(8,128)(2,1)}, bf16[1024,512]{1,0:T(8,128)(2,1)}, u32[]{:S(2)}, u32[]{:S(2)}) collective-permute-start(bf16[1024,512]{1,0:T(8,128)(2,1)} %get-tuple-element.23), channel_id=1, source_target_pairs={{0,1},{1,2},{2,3},{4,5},{5,6},{6,7},{8,9},{9,10},{10,11},{12,13},{... | collective-permute-start | bytes 3145736 | tf_op jit(solution)/shard_map/ppermute | solution.py:83
  16.8 86.5 %collective-permute-start.1 = (bf16[1024,512]{1,0:T(8,128)(2,1)}, bf16[1024,512]{1,0:T(8,128)(2,1)}, u32[]{:S(2)}, u32[]{:S(2)}) collective-permute-start(bf16[1024,512]{1,0:T(8,128)(2,1)} %get-tuple-element.23), channel_id=1, source_target_pairs={{1,0},{2,1},{3,2},{5,4},{6,5},{7,6},{9,8},{10,9},{11,10},{13,12},{... | collective-permute-start | bytes 3145736 | tf_op jit(solution)/shard_map/ppermute | solution.py:84
  26.4 7.8 %collective-permute-start.19 = (f32[256,128]{1,0:T(8,128)S(1)}, f32[256,128]{1,0:T(8,128)S(1)}, u32[]{:S(2)}, u32[]{:S(2)}) collective-permute-start(f32[256,128]{1,0:T(8,128)S(1)} %get-tuple-element.25), channel_id=1, source_target_pairs={{0,192},{64,0},{128,64},{192,128},{1,193},{65,1},{129,65},{193,129... | collective-permute-start | bytes 393224 | tf_op jit(solution)/shard_map/ppermute | solution.py:37
  29.5 9.2 %collective-permute-start.17 = (f32[256,128]{1,0:T(8,128)S(1)}, f32[256,128]{1,0:T(8,128)S(1)}, u32[]{:S(2)}, u32[]{:S(2)}) collective-permute-start(f32[256,128]{1,0:T(8,128)S(1)} %get-tuple-element.24), channel_id=1, source_target_pairs={{0,64},{64,128},{128,192},{192,0},{1,65},{65,129},{129,193},{193,1... | collective-permute-start | bytes 393224 | tf_op jit(solution)/shard_map/ppermute | solution.py:37
  45.4 61.1 %collective-permute-start.5 = (bf16[1024,512]{1,0:T(8,128)(2,1)}, bf16[1024,512]{1,0:T(8,128)(2,1)S(1)}, u32[]{:S(2)}, u32[]{:S(2)}) collective-permute-start(bf16[1024,512]{1,0:T(8,128)(2,1)} %get-tuple-element.22), channel_id=1, source_target_pairs={{1,0},{2,1},{3,2},{5,4},{6,5},{7,6},{9,8},{10,9},{11,10},{13,12},{... | collective-permute-start | bytes 3145736 | tf_op jit(solution)/shard_map/ppermute | solution.py:84
  49.3 8.9 %collective-permute-start.23 = (f32[64,128]{1,0:T(8,128)}, f32[64,128]{1,0:T(8,128)}, u32[]{:S(2)}, u32[]{:S(2)}) collective-permute-start(f32[64,128]{1,0:T(8,128)} %add_add_fusion.3), channel_id=1, source_target_pairs={{0,8},{8,0},{1,9},{9,1},{2,10},{10,2},{3,11},{11,3},{4,12},{12,4},... | collective-permute-start | bytes 98312 | tf_op jit(solution)/shard_map/ppermute | solution.py:23
  67.1 6.5 %collective-permute-start.27 = (f32[256,128]{1,0:T(8,128)S(1)}, f32[256,128]{1,0:T(8,128)}, u32[]{:S(2)}, u32[]{:S(2)}) collective-permute-start(f32[256,128]{1,0:T(8,128)S(1)} %constant_dynamic-update-slice_fusion.6), channel_id=1, source_target_pairs={{0,64},{64,128},{128,192},{192,0},{1,65},{65,129},{129,193},{193,1... | collective-permute-start | bytes 393224 | tf_op jit(solution)/shard_map/ppermute | solution.py:47
  67.2 7.3 %collective-permute-start.28 = (f32[256,128]{1,0:T(8,128)S(1)}, f32[256,128]{1,0:T(8,128)S(1)}, u32[]{:S(2)}, u32[]{:S(2)}) collective-permute-start(f32[256,128]{1,0:T(8,128)S(1)} %constant_dynamic-update-slice_fusion.6), channel_id=1, source_target_pairs={{0,128},{64,192},{128,0},{192,64},{1,129},{65,193},{129,1},{193,65... | collective-permute-start | bytes 393224 | tf_op jit(solution)/shard_map/ppermute | solution.py:47
  73.6 23.7 %collective-permute-start.29 = (f32[256,128]{1,0:T(8,128)S(1)}, f32[256,128]{1,0:T(8,128)S(1)}, u32[]{:S(2)}, u32[]{:S(2)}) collective-permute-start(f32[256,128]{1,0:T(8,128)S(1)} %constant_dynamic-update-slice_fusion.6), channel_id=1, source_target_pairs={{0,192},{64,0},{128,64},{192,128},{1,193},{65,1},{129,65},{193,129... | collective-permute-start | bytes 393224 | tf_op jit(solution)/shard_map/ppermute | solution.py:47
  74.5 40.6 %collective-permute-start.4 = (bf16[1024,512]{1,0:T(8,128)(2,1)}, bf16[1024,512]{1,0:T(8,128)(2,1)S(1)}, u32[]{:S(2)}, u32[]{:S(2)}) collective-permute-start(bf16[1024,512]{1,0:T(8,128)(2,1)} %get-tuple-element.22), channel_id=1, source_target_pairs={{0,1},{1,2},{2,3},{4,5},{5,6},{6,7},{8,9},{9,10},{10,11},{12,13},{... | collective-permute-start | bytes 3145736 | tf_op jit(solution)/shard_map/ppermute | solution.py:83
  97.4 21.7 %collective-permute-start.30 = (f32[1024,128]{1,0:T(8,128)S(1)}, f32[1024,128]{1,0:T(8,128)S(1)}, u32[]{:S(2)}, u32[]{:S(2)}) collective-permute-start(f32[1024,128]{1,0:T(8,128)S(1)} %constant_dynamic-update-slice_fusion.2), channel_id=1, source_target_pairs={{0,4},{4,0},{1,5},{5,1},{2,6},{6,2},{3,7},{7,3},{8,12},{12,8},{9,1... | collective-permute-start | bytes 1572872 | tf_op jit(solution)/shard_map/ppermute | solution.py:47
  105.2 27.1 %collective-permute-start.2 = (bf16[1024,512]{1,0:T(8,128)(2,1)S(1)}, bf16[1024,512]{1,0:T(8,128)(2,1)S(1)}, u32[]{:S(2)}, u32[]{:S(2)}) collective-permute-start(bf16[1024,512]{1,0:T(8,128)(2,1)S(1)} %add_convert_fusion.11), channel_id=1, source_target_pairs={{1,0},{2,1},{3,2},{5,4},{6,5},{7,6},{9,8},{10,9},{11,10},{13,12},{... | collective-permute-start | bytes 3145736 | tf_op jit(solution)/shard_map/ppermute | solution.py:104
  107.0 47.8 %collective-permute-start.6 = (bf16[1024,512]{1,0:T(8,128)(2,1)S(1)}, bf16[1024,512]{1,0:T(8,128)(2,1)S(1)}, u32[]{:S(2)}, u32[]{:S(2)}) collective-permute-start(bf16[1024,512]{1,0:T(8,128)(2,1)S(1)} %add_convert_fusion.9), channel_id=1, source_target_pairs={{1,0},{2,1},{3,2},{5,4},{6,5},{7,6},{9,8},{10,9},{11,10},{13,12},{... | collective-permute-start | bytes 3145736 | tf_op jit(solution)/shard_map/ppermute | solution.py:104
  110.2 48.0 %collective-permute-start.8 = (bf16[1024,512]{1,0:T(8,128)(2,1)S(1)}, bf16[1024,512]{1,0:T(8,128)(2,1)S(1)}, u32[]{:S(2)}, u32[]{:S(2)}) collective-permute-start(bf16[1024,512]{1,0:T(8,128)(2,1)S(1)} %add_convert_fusion.7), channel_id=1, source_target_pairs={{0,1},{1,2},{2,3},{4,5},{5,6},{6,7},{8,9},{9,10},{10,11},{12,13},{... | collective-permute-start | bytes 3145736 | tf_op jit(solution)/shard_map/ppermute | solution.py:101
  115.7 47.1 %collective-permute-start.9 = (bf16[1024,512]{1,0:T(8,128)(2,1)S(1)}, bf16[1024,512]{1,0:T(8,128)(2,1)S(1)}, u32[]{:S(2)}, u32[]{:S(2)}) collective-permute-start(bf16[1024,512]{1,0:T(8,128)(2,1)S(1)} %add_convert_fusion.6), channel_id=1, source_target_pairs={{0,1},{1,2},{2,3},{4,5},{5,6},{6,7},{8,9},{9,10},{10,11},{12,13},{... | collective-permute-start | bytes 3145736 | tf_op jit(solution)/shard_map/ppermute | solution.py:101
  132.9 44.4 %collective-permute-start.3 = (bf16[1024,512]{1,0:T(8,128)(2,1)S(1)}, bf16[1024,512]{1,0:T(8,128)(2,1)S(1)}, u32[]{:S(2)}, u32[]{:S(2)}) collective-permute-start(bf16[1024,512]{1,0:T(8,128)(2,1)S(1)} %add_convert_fusion.10), channel_id=1, source_target_pairs={{1,0},{2,1},{3,2},{5,4},{6,5},{7,6},{9,8},{10,9},{11,10},{13,12},{... | collective-permute-start | bytes 3145736 | tf_op jit(solution)/shard_map/ppermute | solution.py:104
  155.3 44.4 %collective-permute-start.7 = (bf16[1024,512]{1,0:T(8,128)(2,1)S(1)}, bf16[1024,512]{1,0:T(8,128)(2,1)S(1)}, u32[]{:S(2)}, u32[]{:S(2)}) collective-permute-start(bf16[1024,512]{1,0:T(8,128)(2,1)S(1)} %add_convert_fusion.8), channel_id=1, source_target_pairs={{1,0},{2,1},{3,2},{5,4},{6,5},{7,6},{9,8},{10,9},{11,10},{13,12},{... | collective-permute-start | bytes 3145736 | tf_op jit(solution)/shard_map/ppermute | solution.py:104
  158.7 45.0 %collective-permute-start.10 = (bf16[1024,512]{1,0:T(8,128)(2,1)S(1)}, bf16[1024,512]{1,0:T(8,128)(2,1)S(1)}, u32[]{:S(2)}, u32[]{:S(2)}) collective-permute-start(bf16[1024,512]{1,0:T(8,128)(2,1)S(1)} %add_convert_fusion.5), channel_id=1, source_target_pairs={{0,1},{1,2},{2,3},{4,5},{5,6},{6,7},{8,9},{9,10},{10,11},{12,13},{... | collective-permute-start | bytes 3145736 | tf_op jit(solution)/shard_map/ppermute | solution.py:101
  163.3 44.9 %collective-permute-start.11 = (bf16[1024,512]{1,0:T(8,128)(2,1)S(1)}, bf16[1024,512]{1,0:T(8,128)(2,1)S(1)}, u32[]{:S(2)}, u32[]{:S(2)}) collective-permute-start(bf16[1024,512]{1,0:T(8,128)(2,1)S(1)} %add_convert_fusion.4), channel_id=1, source_target_pairs={{0,1},{1,2},{2,3},{4,5},{5,6},{6,7},{8,9},{9,10},{10,11},{12,13},{... | collective-permute-start | bytes 3145736 | tf_op jit(solution)/shard_map/ppermute | solution.py:101
  220.5 35.7 %collective-permute-start.13 = (bf16[1024,512]{1,0:T(8,128)(2,1)}, bf16[1024,512]{1,0:T(8,128)(2,1)S(1)}, u32[]{:S(2)}, u32[]{:S(2)}) collective-permute-start(bf16[1024,512]{1,0:T(8,128)(2,1)} %add_convert_fusion.2), channel_id=1, source_target_pairs={{1,0},{2,1},{3,2},{5,4},{6,5},{7,6},{9,8},{10,9},{11,10},{13,12},{... | collective-permute-start | bytes 3145736 | tf_op jit(solution)/shard_map/ppermute | solution.py:104
  224.5 31.7 %collective-permute-start.12 = (bf16[1024,512]{1,0:T(8,128)(2,1)}, bf16[1024,512]{1,0:T(8,128)(2,1)}, u32[]{:S(2)}, u32[]{:S(2)}) collective-permute-start(bf16[1024,512]{1,0:T(8,128)(2,1)} %add_convert_fusion.3), channel_id=1, source_target_pairs={{0,1},{1,2},{2,3},{4,5},{5,6},{6,7},{8,9},{9,10},{10,11},{12,13},{... | collective-permute-start | bytes 3145736 | tf_op jit(solution)/shard_map/ppermute | solution.py:101
  233.0 35.5 %collective-permute-start.15 = (bf16[1024,512]{1,0:T(8,128)(2,1)}, bf16[1024,512]{1,0:T(8,128)(2,1)}, u32[]{:S(2)}, u32[]{:S(2)}) collective-permute-start(bf16[1024,512]{1,0:T(8,128)(2,1)} %add_convert_fusion), channel_id=1, source_target_pairs={{1,0},{2,1},{3,2},{5,4},{6,5},{7,6},{9,8},{10,9},{11,10},{13,12},{... | collective-permute-start | bytes 3145736 | tf_op jit(solution)/shard_map/ppermute | solution.py:104
  237.0 35.1 %collective-permute-start.14 = (bf16[1024,512]{1,0:T(8,128)(2,1)}, bf16[1024,512]{1,0:T(8,128)(2,1)}, u32[]{:S(2)}, u32[]{:S(2)}) collective-permute-start(bf16[1024,512]{1,0:T(8,128)(2,1)} %add_convert_fusion.1), channel_id=1, source_target_pairs={{0,1},{1,2},{2,3},{4,5},{5,6},{6,7},{8,9},{9,10},{10,11},{12,13},{... | collective-permute-start | bytes 3145736 | tf_op jit(solution)/shard_map/ppermute | solution.py:101
  (30 other events, 310.0 us)

commit v2 on v1

v2 whole, which is shorter than its diff:
```python
import functools

import jax
import jax.numpy as jnp
from jax import lax
from jax.experimental import pallas as pl
from jax.experimental.pallas import tpu as pltpu
from jax.sharding import Mesh, PartitionSpec as P

outer_rate = 0.7
momentum_decay = 0.9
epsilon = 1e-05

PIECES = 2
CONTRACT_ROWS = (((0,), (0,)), ((), ()))
CONTRACT_COLUMNS = (((1,), (1,)), ((), ()))
PLAIN = (((1,), (0,)), ((), ()))
f32, bf16 = jnp.float32, jnp.bfloat16


def dot(a, b, dims=PLAIN):
    return lax.dot_general(a, b, dims, preferred_element_type=f32)


def place(me, mirrored, n):
    return jnp.where(mirrored == 1, n - 1 - me, me)


def pass_on_kernel(n, s, c, inputs, split, me_ref, x_ref, c_ref, *refs):
    there, back = refs[0], refs[1]
    outs = refs[inputs:]
    columns, held, sems = refs[-3:]
    me, mirrored = me_ref[0], me_ref[1]
    rows, block = held.shape[1], columns.shape[3]
    steps = rows // block
    part = rows // split
    ways = ((there, n - s + me, me < s), (back, me + s - n, me > n - 1 - s))

    def some(j):
        return pl.ds(j * block, block)

    def columns_in(d, j):
        first = place(ways[d][1], mirrored, n) * (rows * PIECES) + c * rows + j * block
        source = x_ref.at[:, pl.ds(pl.multiple_of(first, block), block)]
        return pltpu.make_async_copy(source, columns.at[d, j], sems.at[d, j, 0])

    def sum_in(d, j):
        return pltpu.make_async_copy(ways[d][0].at[some(j)], held.at[d, some(j)], sems.at[d, j, 1])

    def sum_out(d, j):
        target = outs[d * split + j * block // part].at[pl.ds(j * block % part, block)]
        return pltpu.make_async_copy(held.at[d, some(j)], target, sems.at[d, j, 2])

    def fetch(d):
        for j in range(steps):
            columns_in(d, j).start()
            sum_in(d, j).start()

    def add(d):
        for j in range(steps):
            columns_in(d, j).wait()
            sum_in(d, j).wait()
            term = dot(columns[d, j], c_ref[...], CONTRACT_ROWS)
            held[d, some(j)] = (held[d, some(j)].astype(f32) + term).astype(bf16)
            sum_out(d, j).start()

    def finish(d):
        for j in range(steps):
            sum_out(d, j).wait()

    for step in (fetch, add, finish):
        for d in range(2):
            pl.when(ways[d][2])(functools.partial(step, d))


def pass_on(s, c, n, me, activations, cotangent, there, back, tokens=(), rider=None, split=1):
    rows, key_width = there.shape
    tokens_here = activations.shape[0]
    block = 256
    any_spec = pl.BlockSpec(memory_space=pl.ANY)
    riders = [] if rider is None else [rider]
    operands = [there, back, *riders, *tokens]
    last = s == n - 1
    outs = [jax.ShapeDtypeStruct((rows // split, key_width), bf16)] * (2 * split)
    outs += [jax.ShapeDtypeStruct(r.shape, r.dtype) for r in riders]
    aliases = {} if last else {3: 0, 4: 1}
    if riders:
        aliases[5] = len(outs) - 1
    return pl.pallas_call(
        functools.partial(pass_on_kernel, n, s, c, len(operands), split),
        out_shape=outs,
        in_specs=[
            pl.BlockSpec(memory_space=pltpu.SMEM),
            any_spec,
            pl.BlockSpec(memory_space=pltpu.VMEM),
        ]
        + [any_spec] * len(operands),
        out_specs=[any_spec] * len(outs),
        scratch_shapes=[
            pltpu.VMEM((2, rows // block, tokens_here, block), bf16),
            pltpu.VMEM((2, rows, key_width), bf16),
            pltpu.SemaphoreType.DMA((2, rows // block, 3)),
        ],
        input_output_aliases=aliases,
        compiler_params=pltpu.CompilerParams(vmem_limit_bytes=56 * 2**20),
        cost_estimate=pl.CostEstimate(
            flops=10**11 if (s, c) == (2, 0) else 0, bytes_accessed=4 * 2**20, transcendentals=0
        ),
    )(me, activations, cotangent, *operands)


def project_kernel(n, factor, tokens, me_ref, x_ref, c_ref, inverse_ref, *refs):
    own, from_left, from_right = refs[:PIECES], [], []
    at = PIECES
    for _ in range(n - 1):
        from_left.append(refs[at : at + PIECES])
        at += PIECES
    for _ in range(n - 1):
        from_right.append(refs[at : at + PIECES])
        at += PIECES
    keys_ref, grad_ref, held, total, adjusted, sems = refs[at + tokens :]
    me, mirrored = me_ref[0], me_ref[1]
    rows = held.shape[1]
    model_width = x_ref.shape[1]
    order = [(o, c) for o in (0, 2, 1, 3) for c in range(PIECES)]

    def fetch(index):
        o, c = order[index]
        slot = index % 4

        def start(ref):
            pltpu.make_async_copy(ref, held.at[slot], sems.at[slot]).start()

        if o == 0:
            start(own[c])
        else:
            pl.when(me >= o)(lambda: start(from_left[o - 1][c]))
            pl.when(me < o)(lambda: start(from_right[n - 1 - o][c]))

    for index in range(3):
        fetch(index)
    cotangent = c_ref[...]
    for index, (o, c) in enumerate(order):
        if index + 3 < len(order):
            fetch(index + 3)
        slot = index % 4
        pltpu.make_async_copy(own[0], held.at[slot], sems.at[slot]).wait()
        owner = place(lax.rem(me - o + n, n), mirrored, n)
        start = pl.multiple_of(owner * (rows * PIECES) + c * rows, 128)
        columns = pl.ds(start, rows)
        part = dot(x_ref[:, columns], held[slot])
        if index == 0:
            total[...] = part
        else:
            total[...] += part
        adjusted[:, columns] = dot(cotangent, held[slot], CONTRACT_COLUMNS)
    inverse = inverse_ref[...]
    keys = total[...] * (inverse * factor)
    keys_ref[...] = keys.astype(bf16)
    mean = jnp.sum(keys * cotangent.astype(f32), axis=1, keepdims=True) * (1.0 / model_width)
    scale = inverse * factor
    take = inverse * inverse * mean
    for start in range(0, model_width, 1024):
        columns = slice(start, start + 1024)
        grad_ref[:, columns] = (
            scale * adjusted[:, columns] - x_ref[:, columns].astype(f32) * take
        ).astype(bf16)


def project(me, activations, key_cotangent, inverse, own, from_left, from_right, factor, waits):
    tokens, model_width = activations.shape
    key_width = key_cotangent.shape[1]
    n = len(from_left) + 1
    rows = own[0].shape[0]
    pieces = list(own)
    pieces += [p for ps in from_left for p in ps] + [p for ps in from_right for p in ps]
    pieces += waits
    vmem = pl.BlockSpec(memory_space=pltpu.VMEM)
    return pl.pallas_call(
        functools.partial(project_kernel, n, factor, len(waits)),
        out_shape=(
            jax.ShapeDtypeStruct((tokens, key_width), bf16),
            jax.ShapeDtypeStruct((tokens, model_width), bf16),
        ),
        in_specs=[pl.BlockSpec(memory_space=pltpu.SMEM), vmem, vmem, vmem]
        + [pl.BlockSpec(memory_space=pl.ANY)] * len(pieces),
        out_specs=(vmem, vmem),
        scratch_shapes=[
            pltpu.VMEM((4, rows, key_width), bf16),
            pltpu.VMEM((tokens, key_width), f32),
            pltpu.VMEM((tokens, model_width), f32),
            pltpu.SemaphoreType.DMA((4,)),
        ],
        compiler_params=pltpu.CompilerParams(vmem_limit_bytes=28 * 2**20),
        cost_estimate=pl.CostEstimate(
            flops=4 * tokens * model_width * key_width,
            bytes_accessed=16 * 2**20,
            transcendentals=0,
        ),
    )(me, activations, key_cotangent, inverse, *pieces)


def weight_kernel(factor, first, x_ref, c_ref, right_ref, left_ref, weight_ref, gain_ref, *refs):
    grad_ref, gain_grad_ref, grad, gain_grad, sems = refs[-5:]
    rows, width = grad.shape
    block = 256
    gain = jnp.broadcast_to(gain_ref[:, first : first + rows].astype(f32) * factor, (128, rows)).T
    copies = []
    for j in range(0, rows, block):
        some, mine = slice(j, j + block), slice(first + j, first + j + block)
        own = dot(x_ref[:, mine], c_ref[...], CONTRACT_ROWS)
        folded = None
        for start in range(0, width, 128):
            lanes = slice(start, start + 128)
            summed = own[:, lanes] + right_ref[some, lanes].astype(f32) + left_ref[some, lanes].astype(f32)
            grad[some, lanes] = (summed * gain[some]).astype(bf16)
            terms = summed * weight_ref[mine, lanes].astype(f32)
            folded = terms if folded is None else folded + terms
        copies.append(pltpu.make_async_copy(grad.at[some], grad_ref.at[mine], sems.at[j // block]))
        copies[-1].start()
        gain_grad[:, some] = jnp.sum(folded.T, axis=0, keepdims=True) * factor
    copies.append(
        pltpu.make_async_copy(
            gain_grad, gain_grad_ref.at[:, first : first + rows], sems.at[rows // block]
        )
    )
    copies[-1].start()
    for copy in copies:
        copy.wait()


def weight_piece(factor, first, columns, cotangent, right, left, weight, gain, so_far):
    shard, key_width = weight.shape
    rows = right.shape[0]
    any_spec = pl.BlockSpec(memory_space=pl.ANY)
    operands = [columns, cotangent, right, left, weight, gain]
    in_specs = [pl.BlockSpec(memory_space=pltpu.VMEM)] * len(operands)
    aliases = {}
    if so_far is not None:
        aliases = {len(operands): 0, len(operands) + 1: 1}
        in_specs += [any_spec, any_spec]
        operands += list(so_far)
    return pl.pallas_call(
        functools.partial(weight_kernel, factor, first),
        out_shape=(
            jax.ShapeDtypeStruct((shard, key_width), bf16),
            jax.ShapeDtypeStruct((1, shard), f32),
        ),
        in_specs=in_specs,
        out_specs=(any_spec, any_spec),
        scratch_shapes=[
            pltpu.VMEM((rows, key_width), bf16),
            pltpu.VMEM((1, rows), f32),
            pltpu.SemaphoreType.DMA((rows // 256 + 1,)),
        ],
        input_output_aliases=aliases,
        compiler_params=pltpu.CompilerParams(vmem_limit_bytes=16 * 2**20),
        cost_estimate=pl.CostEstimate(flops=0, bytes_accessed=4 * 2**20, transcendentals=0),
    )(*operands)


def body(sizes, activations, norm_gain, key_weight, key_cotangent, outer_params, outer_momentum, fragment):
    n = sizes["fsdp"]
    tokens, model_width = activations.shape
    key_width = key_cotangent.shape[1]
    head_size = outer_params.shape[1]
    shard = key_weight.shape[1]
    factor = model_width ** (-0.5)
    weight = key_weight[0]
    mirrored = lax.axis_index("core")
    me = place(lax.axis_index("fsdp"), mirrored, n)
    where_am_i = jnp.stack([me, mirrored]).astype(jnp.int32)
    line = ("core", "fsdp")
    up = [(j, j + 1) for j in range(n - 1)] + [(n + j + 1, n + j) for j in range(n - 1)]
    down = [(j, i) for i, j in up]

    def send(there, back):
        return [lax.ppermute(there, line, up), lax.ppermute(back, line, down)]

    gain = norm_gain[0].astype(f32)[:, None]
    rows = shard // PIECES

    def scaled(weight, c):
        part = slice(c * rows, (c + 1) * rows)
        return (weight[part].astype(f32) * gain[part]).astype(bf16)

    first = scaled(weight, 0)
    first, weight, activations = lax.optimization_barrier((first, weight, activations))
    own, flying = [first], [send(first, first)]

    column_start = fragment[0] % (key_width // head_size) * head_size
    local_block = lax.dynamic_slice_in_dim(weight, column_start, head_size, 1)
    plane = ("x", "y", "core")
    owners = sizes["x"] * sizes["y"] * sizes["core"]
    spread = (owners, shard // owners, head_size)
    delta = (outer_params - local_block.astype(f32)).reshape(spread)

    xfloat = activations.astype(f32)
    inverse = lax.rsqrt(jnp.mean(xfloat * xfloat, axis=1, keepdims=True) + epsilon)
    cotangent = (key_cotangent.astype(f32) * inverse).astype(bf16)
    weight, delta, cotangent = lax.optimization_barrier((weight, delta, cotangent))
    for c in range(1, PIECES):
        piece = scaled(weight, c)
        piece, delta = lax.optimization_barrier((piece, delta))
        own.append(piece)
        flying.append(send(piece, piece))
    delta = lax.all_to_all(delta, plane, 0, 0, tiled=True)

    from_near, from_far, last_parts = [], [], []
    before = ()
    for s in range(1, n):
        passed_there, passed_back, following = [], [], []
        for c in range(PIECES):
            there, back = flying[c]
            last = s == n - 1
            split = 1
            tokens, rider = list(before), None
            if (s, c) == (1, 1):
                total = jnp.sum(delta, axis=0)
            if (s, c) in ((1, 1), (2, 1)):
                rider = total
            if (s, c) == (2, 0):
                tokens.append(total)
            outs = pass_on(
                s, c, n, where_am_i, activations, cotangent, there, back, tokens, rider, split
            )
            if (s, c) == (1, 1):
                total = outs[-1] + lax.ppermute(outs[-1], "zh", [(0, 1), (1, 0)])
            if (s, c) == (2, 1):
                delta = jnp.broadcast_to(outs[-1][None], spread)
                delta = lax.all_to_all(delta, plane, 0, 0, tiled=True)
            before = outs[: 2 * split]
            passed_there.append(there if last else outs[0])
            passed_back.append(back if last else outs[1])
            following += [send(*pair) for pair in zip(outs[:split], outs[split : 2 * split])]
        flying = following
        from_near.append(passed_there)
        from_far.append(passed_back)

    keys, input_grad = project(
        where_am_i, activations, key_cotangent, inverse, own, from_near, from_far, factor, list(before)
    )
    keys, delta = lax.optimization_barrier((keys, delta))

    replicas = sizes["x"] * sizes["y"] * sizes["zh"] * sizes["core"]
    increment = delta.reshape(outer_params.shape) / replicas
    new_momentum = momentum_decay * outer_momentum + increment
    new_params = outer_params - outer_rate * (increment + momentum_decay * new_momentum)

    columns = lax.dynamic_slice_in_dim(activations, lax.axis_index("fsdp") * shard, shard, 1)
    so_far, start = None, 0
    for right, left in flying:
        so_far = weight_piece(
            factor, start, columns, cotangent, right, left, weight, norm_gain, so_far
        )
        start += right.shape[0]
    weight_grad, gain_grad = so_far
    return (keys, input_grad, weight_grad[None], gain_grad, new_params, new_momentum)


def solution(mesh):
    sizes = {"x": 4, "y": 4, "zh": 2, "core": 2, "fsdp": 4}
    fine = Mesh(mesh.devices.reshape(tuple(sizes.values())), tuple(sizes))
    rep = ("x", "y", "zh", "core")
    both = rep + ("fsdp",)
    in_specs = (
        P(both, None),
        P(rep, "fsdp"),
        P(rep, "fsdp", None),
        P(both, None),
        P("fsdp", None),
        P("fsdp", None),
        P(),
    )
    out_specs = (
        P(both, None),
        P(both, None),
        P(rep, "fsdp", None),
        P(rep, "fsdp"),
        P("fsdp", None),
        P("fsdp", None),
    )

    def local(*args):
        return body(sizes, *args)

    return jax.shard_map(local, mesh=fine, in_specs=in_specs, out_specs=out_specs, check_vma=False)
```

time: 282 us -> 196 us (0.70)
  waiting for transfers between devices: 96.7 us -> 42.5 us
  Pallas kernels: 0 us -> 41.6 us
  matrix products: 37.1 us -> 0 us
  local copies, waits for them, and re-layouts: 24.1 us -> 12.3 us
  other arithmetic: 28.5 us -> 17.2 us
  starting transfers between devices: 89.8 us -> 79.3 us
    ppermute x31 -> x17, waiting for transfers between devices: 96.7 us -> 37.4 us  [the longest x16 22.5 us: send(): return [lax.ppermute(there, line, up), lax.ppermute(back, line, down)]]
    pallas_call x0 -> x9, Pallas kernels: none -> 41.6 us  [the longest x6 24 us: pass_on(): pl.pallas_call(functools.partial(pass_on_kernel, n, s, c, len(operands),...]
    dot_general x16 -> x0, matrix products: 37.1 us -> none  [dot(): return lax.dot_general(a, b, dims, preferred_element_type=f32)]
    ppermute x31 -> x17, starting transfers between devices: 89.8 us -> 61.9 us  [the longest x16 55 us: send(): return [lax.ppermute(there, line, up), lax.ppermute(back, line, down)]]
    all_to_all x0 -> x2, starting transfers between devices: none -> 17.4 us  [body(): delta = lax.all_to_all(delta, plane, 0, 0, tiled=True)]
    dynamic_update_slice x8 -> x0, other arithmetic: 12 us -> none  [the longest x6 9.44 us: body(): lax.dynamic_update_slice_in_dim(whole, piece, (me - o + n) % n * shard +...]
    unnamed x50 -> x34, local copies, waits for them, and re-layouts: 16.1 us -> 7.29 us
    all_to_all x0 -> x2, waiting for transfers between devices: none -> 5.1 us  [body(): delta = lax.all_to_all(delta, plane, 0, 0, tiled=True)]
  transfers between devices with their start and end apart: 31 -> 19, of which waited for: 15 -> 8; matrix products, arithmetic and copies ran while one was open for 24% -> 10% of each run, Pallas kernels for 0% -> 20%
where the time goes in v2:
time: 196 us; the launch traced here: 195 us
  starting transfers between devices  79.3 us (40%)
  waiting for transfers between devices  42.5 us (22%)
  Pallas kernels  41.6 us (21%)
  other arithmetic  17.2 us (9%)
  local copies, waits for them, and re-layouts  12.3 us (6%)
    ppermute x16, starting transfers between devices, send(): return [lax.ppermute(there, line, up), lax.ppermute(back, line, down)]  55 us
    pallas_call x6, Pallas kernels, pass_on(): pl.pallas_call(functools.partial(pass_on_kernel, n, s, c, len(operands),...  24 us
    ppermute x16, waiting for transfers between devices, send(): return [lax.ppermute(there, line, up), lax.ppermute(back, line, down)]  22.5 us
    all_to_all x2, starting transfers between devices, body(): delta = lax.all_to_all(delta, plane, 0, 0, tiled=True)  17.4 us
    ppermute x1, waiting for transfers between devices, body(): total = outs[-1] + lax.ppermute(outs[-1], 'zh', [(0, 1), (1, 0)])  14.8 us
    pallas_call x1, Pallas kernels, project(): pl.pallas_call(functools.partial(project_kernel, n, factor, len(waits)),...  11.4 us
    unnamed x34, local copies, waits for them, and re-layouts  7.29 us
    ppermute x1, starting transfers between devices, body(): total = outs[-1] + lax.ppermute(outs[-1], 'zh', [(0, 1), (1, 0)])  6.92 us
  transfers between devices with their start and end apart: 19, of which 8 were waited for; matrix products, arithmetic and copies ran while one was open for 10% of the time, Pallas kernels for 20%

profile of v2, /device:TPU:1, one launch (start us, length us, event | category | flops | bytes accessed | tf_op | source)
XLA Modules:
  0.0 194.6 jit_solution(16180116824416871307)
XLA Ops:
  5.1 6.0 %collective-permute-start.1 = (bf16[1024,512]{1,0:T(8,128)(2,1)}, bf16[1024,512]{1,0:T(8,128)(2,1)}, u32[]{:S(2)}, u32[]{:S(2)}) collective-permute-start(bf16[1024,512]{1,0:T(8,128)(2,1)} %fusion.refs_0_), channel_id=1, source_target_pairs={{1,0},{2,1},{3,2},{4,5},{5,6},{6,7},{9,8},{10,9},{11,10},{12,13},{... | collective-permute-start | bytes 3145736 | tf_op jit(solution)/shard_map/ppermute | solution.py:278
  20.8 5.0 %collective-permute-start.3 = (bf16[1024,512]{1,0:T(8,128)(2,1)}, bf16[1024,512]{1,0:T(8,128)(2,1)}, u32[]{:S(2)}, u32[]{:S(2)}) collective-permute-start(bf16[1024,512]{1,0:T(8,128)(2,1)} %multiply_convert_fusion.refs_1_), channel_id=1, source_target_pairs={{1,0},{2,1},{3,2},{4,5},{5,6},{6,7},{9,8},{10,9},{11,10},{12,13},{... | collective-permute-start | bytes 3145736 | tf_op jit(solution)/shard_map/ppermute | solution.py:278
  25.8 7.3 %all-to-all-start = ((f32[32,64,128]{2,1,0:T(8,128)}), f32[32,64,128]{2,1,0:T(8,128)}, u32[]{:S(2)}, u32[]{:S(2)}) async-start(f32[32,64,128]{2,1,0:T(8,128)} %bitcast.27), calls=%async_computation | async-start | bytes 2097152 | tf_op jit(solution)/shard_map/all_to_all | solution.py:307
  34.7 3.9 %shard_map.118 = (bf16[1024,512]{1,0:T(8,128)(2,1)}, bf16[1024,512]{1,0:T(8,128)(2,1)}) custom-call(s32[2]{0:T(128)} %pad_add_fusion.me_ref, bf16[256,8192]{1,0:T(8,128)(2,1)} %x_ref.6, bf16[256,512]{1,0:T(8,128)(2,1)} %multiply_convert_fusion.1.c_ref, bf16[1024,512]{1,0:T(8,128)(2,1)} %copy-done.7, ...), custom_call_target="tpu_custom_call", output_to_operand_aliasing={{0}: (3, {}), {1}: (4, {})} | custom-call | bytes 4194304 | tf_op jit(solution)/shard_map/pallas_call | solution.py:89
  39.9 5.0 %collective-permute-start.5 = (bf16[1024,512]{1,0:T(8,128)(2,1)}, bf16[1024,512]{1,0:T(8,128)(2,1)}, u32[]{:S(2)}, u32[]{:S(2)}) collective-permute-start(bf16[1024,512]{1,0:T(8,128)(2,1)} %get-tuple-element.45.refs_4_.refs_8_), channel_id=1, source_target_pairs={{1,0},{2,1},{3,2},{4,5},{5,6},{6,7},{9,8},{10,9},{11,10},{12,13},{... | collective-permute-start | bytes 3145736 | tf_op jit(solution)/shard_map/ppermute | solution.py:278
  44.9 5.1 %all-to-all-done = f32[32,64,128]{2,1,0:T(8,128)} async-done(((f32[32,64,128]{2,1,0:T(8,128)}), f32[32,64,128]{2,1,0:T(8,128)}, u32[]{:S(2)}, u32[]{:S(2)}) %all-to-all-start) | async-done | bytes 1048608 | tf_op jit(solution)/shard_map/all_to_all | solution.py:307
  51.9 3.9 %collective-permute-done.3.refs_1_ = bf16[1024,512]{1,0:T(8,128)(2,1)} collective-permute-done((bf16[1024,512]{1,0:T(8,128)(2,1)}, bf16[1024,512]{1,0:T(8,128)(2,1)}, u32[]{:S(2)}, u32[]{:S(2)}) %collective-permute-start.3) | collective-permute-done | bytes 1048608 | tf_op jit(solution)/shard_map/ppermute | solution.py:278
  55.8 3.9 %shard_map.119 = (bf16[1024,512]{1,0:T(8,128)(2,1)}, bf16[1024,512]{1,0:T(8,128)(2,1)}, f32[64,128]{1,0:T(8,128)}) custom-call(s32[2]{0:T(128)} %pad_add_fusion.me_ref, bf16[256,8192]{1,0:T(8,128)(2,1)} %x_ref.6, bf16[256,512]{1,0:T(8,128)(2,1)} %multiply_convert_fusion.1.c_ref, ...), custom_call_target="tpu_custom_call", output_to_operand_aliasing={{0}: (3, {}), {1}: (4, {}), {2}: (5, {})} | custom-call | bytes 4194304 | tf_op jit(solution)/shard_map/pallas_call | solution.py:89
  59.8 6.9 %collective-permute-start.6 = (f32[64,128]{1,0:T(8,128)}, f32[64,128]{1,0:T(8,128)S(1)}, u32[]{:S(2)}, u32[]{:S(2)}) collective-permute-start(f32[64,128]{1,0:T(8,128)} %get-tuple-element.48), channel_id=1, source_target_pairs={{0,8},{8,0},{1,9},{9,1},{2,10},{10,2},{3,11},{11,3},{4,12},{12,4},... | collective-permute-start | bytes 98312 | tf_op jit(solution)/shard_map/ppermute | solution.py:328
  68.0 4.1 %collective-permute-start.8 = (bf16[1024,512]{1,0:T(8,128)(2,1)}, bf16[1024,512]{1,0:T(8,128)(2,1)S(1)}, u32[]{:S(2)}, u32[]{:S(2)}) collective-permute-start(bf16[1024,512]{1,0:T(8,128)(2,1)} %get-tuple-element.47.refs_3_.refs_9_), channel_id=1, source_target_pairs={{1,0},{2,1},{3,2},{4,5},{5,6},{6,7},{9,8},{10,9},{11,10},{12,13},{... | collective-permute-start | bytes 3145736 | tf_op jit(solution)/shard_map/ppermute | solution.py:278
  72.0 14.8 %collective-permute-done.6 = f32[64,128]{1,0:T(8,128)S(1)} collective-permute-done((f32[64,128]{1,0:T(8,128)}, f32[64,128]{1,0:T(8,128)S(1)}, u32[]{:S(2)}, u32[]{:S(2)}) %collective-permute-start.6) | collective-permute-done | bytes 32800 | tf_op jit(solution)/shard_map/ppermute | solution.py:328
  88.3 3.9 %shard_map.120 = (bf16[1024,512]{1,0:T(8,128)(2,1)}, bf16[1024,512]{1,0:T(8,128)(2,1)}) custom-call(s32[2]{0:T(128)} %pad_add_fusion.me_ref, bf16[256,8192]{1,0:T(8,128)(2,1)} %x_ref.6, bf16[256,512]{1,0:T(8,128)(2,1)} %multiply_convert_fusion.1.c_ref, ...), custom_call_target="tpu_custom_call", output_to_operand_aliasing={{0}: (3, {}), {1}: (4, {})} | custom-call | flops 99999997952 | bytes 4194304 | tf_op jit(solution)/shard_map/pallas_call | solution.py:89
  93.5 5.0 %collective-permute-start.11 = (bf16[1024,512]{1,0:T(8,128)(2,1)}, bf16[1024,512]{1,0:T(8,128)(2,1)}, u32[]{:S(2)}, u32[]{:S(2)}) collective-permute-start(bf16[1024,512]{1,0:T(8,128)(2,1)} %get-tuple-element.50.refs_4_.refs_10_), channel_id=1, source_target_pairs={{1,0},{2,1},{3,2},{4,5},{5,6},{6,7},{9,8},{10,9},{11,10},{12,13},{... | collective-permute-start | bytes 3145736 | tf_op jit(solution)/shard_map/ppermute | solution.py:278
  103.2 3.9 %shard_map.121 = (bf16[1024,512]{1,0:T(8,128)(2,1)}, bf16[1024,512]{1,0:T(8,128)(2,1)}, f32[64,128]{1,0:T(8,128)}) custom-call(s32[2]{0:T(128)} %pad_add_fusion.me_ref, bf16[256,8192]{1,0:T(8,128)(2,1)} %x_ref.6, bf16[256,512]{1,0:T(8,128)(2,1)} %multiply_convert_fusion.1.c_ref, ...), custom_call_target="tpu_custom_call", output_to_operand_aliasing={{0}: (3, {}), {1}: (4, {}), {2}: (5, {})} | custom-call | bytes 4194304 | tf_op jit(solution)/shard_map/pallas_call | solution.py:89
  108.4 5.7 %collective-permute-start.12 = (bf16[1024,512]{1,0:T(8,128)(2,1)}, bf16[1024,512]{1,0:T(8,128)(2,1)}, u32[]{:S(2)}, u32[]{:S(2)}) collective-permute-start(bf16[1024,512]{1,0:T(8,128)(2,1)} %get-tuple-element.52.refs_3_.refs_11_), channel_id=1, source_target_pairs={{1,0},{2,1},{3,2},{4,5},{5,6},{6,7},{9,8},{10,9},{11,10},{12,13},{... | collective-permute-start | bytes 3145736 | tf_op jit(solution)/shard_map/ppermute | solution.py:278
  116.0 10.2 %all-to-all-start.1 = ((f32[32,64,128]{2,1,0:T(8,128)}), f32[32,64,128]{2,1,0:T(8,128)}, u32[]{:S(2)}, u32[]{:S(2)}) async-start(f32[32,64,128]{2,1,0:T(8,128)} %broadcast_in_dim.4), calls=%async_computation.1 | async-start | bytes 2097152 | tf_op jit(solution)/shard_map/all_to_all | solution.py:331
  128.7 3.9 %shard_map.122 = (bf16[1024,512]{1,0:T(8,128)(2,1)}, bf16[1024,512]{1,0:T(8,128)(2,1)}) custom-call(s32[2]{0:T(128)} %pad_add_fusion.me_ref, bf16[256,8192]{1,0:T(8,128)(2,1)} %x_ref.6, bf16[256,512]{1,0:T(8,128)(2,1)} %multiply_convert_fusion.1.c_ref, bf16[1024,512]{1,0:T(8,128)(2,1)} %collective-permute-done.9.refs_0_.refs_6_, ...), custom_call_target="tpu_custom_call" | custom-call | bytes 4194304 | tf_op jit(solution)/shard_map/pallas_call | solution.py:89
  133.9 7.0 %collective-permute-start.16 = (bf16[1024,512]{1,0:T(8,128)(2,1)}, bf16[1024,512]{1,0:T(8,128)(2,1)}, u32[]{:S(2)}, u32[]{:S(2)}) collective-permute-start(bf16[1024,512]{1,0:T(8,128)(2,1)} %get-tuple-element.54.refs_3_), channel_id=1, source_target_pairs={{1,0},{2,1},{3,2},{4,5},{5,6},{6,7},{9,8},{10,9},{11,10},{12,13},{... | collective-permute-start | bytes 3145736 | tf_op jit(solution)/shard_map/ppermute | solution.py:278
  142.1 5.0 %collective-permute-done.12.refs_1_.refs_13_ = bf16[1024,512]{1,0:T(8,128)(2,1)} collective-permute-done((bf16[1024,512]{1,0:T(8,128)(2,1)}, bf16[1024,512]{1,0:T(8,128)(2,1)}, u32[]{:S(2)}, u32[]{:S(2)}) %collective-permute-start.12) | collective-permute-done | bytes 1048608 | tf_op jit(solution)/shard_map/ppermute | solution.py:278
  147.1 4.3 %shard_map.123 = (bf16[1024,512]{1,0:T(8,128)(2,1)}, bf16[1024,512]{1,0:T(8,128)(2,1)}) custom-call(s32[2]{0:T(128)} %pad_add_fusion.me_ref, bf16[256,8192]{1,0:T(8,128)(2,1)} %x_ref.6, bf16[256,512]{1,0:T(8,128)(2,1)} %multiply_convert_fusion.1.c_ref, bf16[1024,512]{1,0:T(8,128)(2,1)} %collective-permute-done.10.refs_0_.refs_7_, ...), custom_call_target="tpu_custom_call" | custom-call | bytes 4194304 | tf_op jit(solution)/shard_map/pallas_call | solution.py:89
  152.7 6.9 %collective-permute-start.14 = (bf16[1024,512]{1,0:T(8,128)(2,1)}, bf16[1024,512]{1,0:T(8,128)(2,1)}, u32[]{:S(2)}, u32[]{:S(2)}) collective-permute-start(bf16[1024,512]{1,0:T(8,128)(2,1)} %get-tuple-element.56.refs_15_), channel_id=1, source_target_pairs={{1,0},{2,1},{3,2},{4,5},{5,6},{6,7},{9,8},{10,9},{11,10},{12,13},{... | collective-permute-start | bytes 3145736 | tf_op jit(solution)/shard_map/ppermute | solution.py:278
  164.5 11.4 %shard_map.124 = (bf16[256,512]{1,0:T(8,128)(2,1)}, bf16[256,8192]{1,0:T(8,128)(2,1)}) custom-call(s32[2]{0:T(128)S(1)} %copy-done.14, bf16[256,8192]{1,0:T(8,128)(2,1)S(1)} %copy-done, bf16[256,512]{1,0:T(8,128)(2,1)S(1)} %copy-done.10, f32[256,1]{1,0:T(8,128)S(1)} %copy.25.inverse_ref, bf16[1024,512]{1,0:T(8,128)(2,1)} %fusion.refs_0_, ...), custom_call_target="tpu_custom_call" | custom-call | flops 4294967296 | bytes 16777216 | tf_op jit(solution)/shard_map/pallas_call | solution.py:179
  182.6 4.5 %collective-permute-done.13.right_ref = bf16[1024,512]{1,0:T(8,128)(2,1)} collective-permute-done((bf16[1024,512]{1,0:T(8,128)(2,1)}, bf16[1024,512]{1,0:T(8,128)(2,1)}, u32[]{:S(2)}, u32[]{:S(2)}) %collective-permute-start.13) | collective-permute-done | bytes 1048608 | tf_op jit(solution)/shard_map/ppermute | solution.py:278
  187.1 4.2 %collective-permute-done.14.left_ref = bf16[1024,512]{1,0:T(8,128)(2,1)} collective-permute-done((bf16[1024,512]{1,0:T(8,128)(2,1)}, bf16[1024,512]{1,0:T(8,128)(2,1)}, u32[]{:S(2)}, u32[]{:S(2)}) %collective-permute-start.14) | collective-permute-done | bytes 1048608 | tf_op jit(solution)/shard_map/ppermute | solution.py:278
  (72 shorter events, 51.0 us)
Async XLA Ops:
  3.8 29.9 %collective-permute-start = (bf16[1024,512]{1,0:T(8,128)(2,1)}, bf16[1024,512]{1,0:T(8,128)(2,1)S(1)}, u32[]{:S(2)}, u32[]{:S(2)}) collective-permute-start(bf16[1024,512]{1,0:T(8,128)(2,1)} %fusion.refs_0_), channel_id=1, source_target_pairs={{0,1},{1,2},{2,3},{5,4},{6,5},{7,6},{8,9},{9,10},{10,11},{13,12},{... | collective-permute-start | bytes 3145736 | tf_op jit(solution)/shard_map/ppermute | solution.py:278
  5.1 28.6 %collective-permute-start.1 = (bf16[1024,512]{1,0:T(8,128)(2,1)}, bf16[1024,512]{1,0:T(8,128)(2,1)}, u32[]{:S(2)}, u32[]{:S(2)}) collective-permute-start(bf16[1024,512]{1,0:T(8,128)(2,1)} %fusion.refs_0_), channel_id=1, source_target_pairs={{1,0},{2,1},{3,2},{4,5},{5,6},{6,7},{9,8},{10,9},{11,10},{12,13},{... | collective-permute-start | bytes 3145736 | tf_op jit(solution)/shard_map/ppermute | solution.py:278
  11.8 4.1 %copy-start.1 = (bf16[1,2048,512]{2,1,0:T(8,128)(2,1)S(1)}, bf16[1,2048,512]{2,1,0:T(8,128)(2,1)}, u32[]{:S(2)}) copy-start(bf16[1,2048,512]{2,1,0:T(8,128)(2,1)} %param.9) | copy-start | bytes 6291460
  19.5 32.4 %collective-permute-start.2 = (bf16[1024,512]{1,0:T(8,128)(2,1)}, bf16[1024,512]{1,0:T(8,128)(2,1)}, u32[]{:S(2)}, u32[]{:S(2)}) collective-permute-start(bf16[1024,512]{1,0:T(8,128)(2,1)} %multiply_convert_fusion.refs_1_), channel_id=1, source_target_pairs={{0,1},{1,2},{2,3},{5,4},{6,5},{7,6},{8,9},{9,10},{10,11},{13,12},{... | collective-permute-start | bytes 3145736 | tf_op jit(solution)/shard_map/ppermute | solution.py:278
  20.8 35.0 %collective-permute-start.3 = (bf16[1024,512]{1,0:T(8,128)(2,1)}, bf16[1024,512]{1,0:T(8,128)(2,1)}, u32[]{:S(2)}, u32[]{:S(2)}) collective-permute-start(bf16[1024,512]{1,0:T(8,128)(2,1)} %multiply_convert_fusion.refs_1_), channel_id=1, source_target_pairs={{1,0},{2,1},{3,2},{4,5},{5,6},{6,7},{9,8},{10,9},{11,10},{12,13},{... | collective-permute-start | bytes 3145736 | tf_op jit(solution)/shard_map/ppermute | solution.py:278
  25.8 24.2 %all-to-all-start = ((f32[32,64,128]{2,1,0:T(8,128)}), f32[32,64,128]{2,1,0:T(8,128)}, u32[]{:S(2)}, u32[]{:S(2)}) async-start(f32[32,64,128]{2,1,0:T(8,128)} %bitcast.27), calls=%async_computation | async-start | bytes 2097152 | tf_op jit(solution)/shard_map/all_to_all | solution.py:307
  38.6 49.6 %collective-permute-start.4 = (bf16[1024,512]{1,0:T(8,128)(2,1)}, bf16[1024,512]{1,0:T(8,128)(2,1)}, u32[]{:S(2)}, u32[]{:S(2)}) collective-permute-start(bf16[1024,512]{1,0:T(8,128)(2,1)} %get-tuple-element.43.refs_3_.refs_2_), channel_id=1, source_target_pairs={{0,1},{1,2},{2,3},{5,4},{6,5},{7,6},{8,9},{9,10},{10,11},{13,12},{... | collective-permute-start | bytes 3145736 | tf_op jit(solution)/shard_map/ppermute | solution.py:278
  39.9 48.3 %collective-permute-start.5 = (bf16[1024,512]{1,0:T(8,128)(2,1)}, bf16[1024,512]{1,0:T(8,128)(2,1)}, u32[]{:S(2)}, u32[]{:S(2)}) collective-permute-start(bf16[1024,512]{1,0:T(8,128)(2,1)} %get-tuple-element.45.refs_4_.refs_8_), channel_id=1, source_target_pairs={{1,0},{2,1},{3,2},{4,5},{5,6},{6,7},{9,8},{10,9},{11,10},{12,13},{... | collective-permute-start | bytes 3145736 | tf_op jit(solution)/shard_map/ppermute | solution.py:278
  59.8 27.1 %collective-permute-start.6 = (f32[64,128]{1,0:T(8,128)}, f32[64,128]{1,0:T(8,128)S(1)}, u32[]{:S(2)}, u32[]{:S(2)}) collective-permute-start(f32[64,128]{1,0:T(8,128)} %get-tuple-element.48), channel_id=1, source_target_pairs={{0,8},{8,0},{1,9},{9,1},{2,10},{10,2},{3,11},{11,3},{4,12},{12,4},... | collective-permute-start | bytes 98312 | tf_op jit(solution)/shard_map/ppermute | solution.py:328
  66.7 31.8 %collective-permute-start.7 = (bf16[1024,512]{1,0:T(8,128)(2,1)}, bf16[1024,512]{1,0:T(8,128)(2,1)S(1)}, u32[]{:S(2)}, u32[]{:S(2)}) collective-permute-start(bf16[1024,512]{1,0:T(8,128)(2,1)} %get-tuple-element.46.refs_2_.refs_3_), channel_id=1, source_target_pairs={{0,1},{1,2},{2,3},{5,4},{6,5},{7,6},{8,9},{9,10},{10,11},{13,12},{... | collective-permute-start | bytes 3145736 | tf_op jit(solution)/shard_map/ppermute | solution.py:278
  68.0 34.2 %collective-permute-start.8 = (bf16[1024,512]{1,0:T(8,128)(2,1)}, bf16[1024,512]{1,0:T(8,128)(2,1)S(1)}, u32[]{:S(2)}, u32[]{:S(2)}) collective-permute-start(bf16[1024,512]{1,0:T(8,128)(2,1)} %get-tuple-element.47.refs_3_.refs_9_), channel_id=1, source_target_pairs={{1,0},{2,1},{3,2},{4,5},{5,6},{6,7},{9,8},{10,9},{11,10},{12,13},{... | collective-permute-start | bytes 3145736 | tf_op jit(solution)/shard_map/ppermute | solution.py:278
  92.2 36.5 %collective-permute-start.9 = (bf16[1024,512]{1,0:T(8,128)(2,1)}, bf16[1024,512]{1,0:T(8,128)(2,1)}, u32[]{:S(2)}, u32[]{:S(2)}) collective-permute-start(bf16[1024,512]{1,0:T(8,128)(2,1)} %get-tuple-element.49.refs_3_.refs_4_), channel_id=1, source_target_pairs={{0,1},{1,2},{2,3},{5,4},{6,5},{7,6},{8,9},{9,10},{10,11},{13,12},{... | collective-permute-start | bytes 3145736 | tf_op jit(solution)/shard_map/ppermute | solution.py:278
  93.5 35.2 %collective-permute-start.11 = (bf16[1024,512]{1,0:T(8,128)(2,1)}, bf16[1024,512]{1,0:T(8,128)(2,1)}, u32[]{:S(2)}, u32[]{:S(2)}) collective-permute-start(bf16[1024,512]{1,0:T(8,128)(2,1)} %get-tuple-element.50.refs_4_.refs_10_), channel_id=1, source_target_pairs={{1,0},{2,1},{3,2},{4,5},{5,6},{6,7},{9,8},{10,9},{11,10},{12,13},{... | collective-permute-start | bytes 3145736 | tf_op jit(solution)/shard_map/ppermute | solution.py:278
  98.5 3.7 %copy-start.3 = (bf16[1024,512]{1,0:T(8,128)(2,1)}, bf16[1024,512]{1,0:T(8,128)(2,1)S(1)}, u32[]{:S(2)}) copy-start(bf16[1024,512]{1,0:T(8,128)(2,1)S(1)} %collective-permute-done.7.refs_0_) | copy-start | bytes 3145732
  107.1 35.0 %collective-permute-start.10 = (bf16[1024,512]{1,0:T(8,128)(2,1)}, bf16[1024,512]{1,0:T(8,128)(2,1)}, u32[]{:S(2)}, u32[]{:S(2)}) collective-permute-start(bf16[1024,512]{1,0:T(8,128)(2,1)} %get-tuple-element.51.refs_2_.refs_5_), channel_id=1, source_target_pairs={{0,1},{1,2},{2,3},{5,4},{6,5},{7,6},{8,9},{9,10},{10,11},{13,12},{... | collective-permute-start | bytes 3145736 | tf_op jit(solution)/shard_map/ppermute | solution.py:278
  108.4 38.7 %collective-permute-start.12 = (bf16[1024,512]{1,0:T(8,128)(2,1)}, bf16[1024,512]{1,0:T(8,128)(2,1)}, u32[]{:S(2)}, u32[]{:S(2)}) collective-permute-start(bf16[1024,512]{1,0:T(8,128)(2,1)} %get-tuple-element.52.refs_3_.refs_11_), channel_id=1, source_target_pairs={{1,0},{2,1},{3,2},{4,5},{5,6},{6,7},{9,8},{10,9},{11,10},{12,13},{... | collective-permute-start | bytes 3145736 | tf_op jit(solution)/shard_map/ppermute | solution.py:278
  116.0 59.9 %all-to-all-start.1 = ((f32[32,64,128]{2,1,0:T(8,128)}), f32[32,64,128]{2,1,0:T(8,128)}, u32[]{:S(2)}, u32[]{:S(2)}) async-start(f32[32,64,128]{2,1,0:T(8,128)} %broadcast_in_dim.4), calls=%async_computation.1 | async-start | bytes 2097152 | tf_op jit(solution)/shard_map/all_to_all | solution.py:331
  132.6 46.8 %collective-permute-start.15 = (bf16[1024,512]{1,0:T(8,128)(2,1)}, bf16[1024,512]{1,0:T(8,128)(2,1)}, u32[]{:S(2)}, u32[]{:S(2)}) collective-permute-start(bf16[1024,512]{1,0:T(8,128)(2,1)} %get-tuple-element.53.refs_2_), channel_id=1, source_target_pairs={{0,1},{1,2},{2,3},{5,4},{6,5},{7,6},{8,9},{9,10},{10,11},{13,12},{... | collective-permute-start | bytes 3145736 | tf_op jit(solution)/shard_map/ppermute | solution.py:278
  133.9 25.7 %copy-start.4 = (bf16[1024,512]{1,0:T(8,128)(2,1)S(1)}, bf16[1024,512]{1,0:T(8,128)(2,1)}, u32[]{:S(2)}) copy-start(bf16[1024,512]{1,0:T(8,128)(2,1)} %get-tuple-element.51.refs_2_.refs_5_) | copy-start | bytes 3145732
  133.9 25.7 %copy-start.14 = (s32[2]{0:T(128)S(1)}, s32[2]{0:T(128)}, u32[]{:S(2)}) copy-start(s32[2]{0:T(128)} %pad_add_fusion.me_ref) | copy-start | bytes 28
  133.9 45.5 %collective-permute-start.16 = (bf16[1024,512]{1,0:T(8,128)(2,1)}, bf16[1024,512]{1,0:T(8,128)(2,1)}, u32[]{:S(2)}, u32[]{:S(2)}) collective-permute-start(bf16[1024,512]{1,0:T(8,128)(2,1)} %get-tuple-element.54.refs_3_), channel_id=1, source_target_pairs={{1,0},{2,1},{3,2},{4,5},{5,6},{6,7},{9,8},{10,9},{11,10},{12,13},{... | collective-permute-start | bytes 3145736 | tf_op jit(solution)/shard_map/ppermute | solution.py:278
  147.1 12.5 %copy-start = (bf16[256,8192]{1,0:T(8,128)(2,1)S(1)}, bf16[256,8192]{1,0:T(8,128)(2,1)}, u32[]{:S(2)}) copy-start(bf16[256,8192]{1,0:T(8,128)(2,1)} %x_ref.6) | copy-start | bytes 12582916
  151.4 35.6 %collective-permute-start.13 = (bf16[1024,512]{1,0:T(8,128)(2,1)}, bf16[1024,512]{1,0:T(8,128)(2,1)}, u32[]{:S(2)}, u32[]{:S(2)}) collective-permute-start(bf16[1024,512]{1,0:T(8,128)(2,1)} %get-tuple-element.55.refs_14_), channel_id=1, source_target_pairs={{0,1},{1,2},{2,3},{5,4},{6,5},{7,6},{8,9},{9,10},{10,11},{13,12},{... | collective-permute-start | bytes 3145736 | tf_op jit(solution)/shard_map/ppermute | solution.py:278
  152.7 38.6 %collective-permute-start.14 = (bf16[1024,512]{1,0:T(8,128)(2,1)}, bf16[1024,512]{1,0:T(8,128)(2,1)}, u32[]{:S(2)}, u32[]{:S(2)}) collective-permute-start(bf16[1024,512]{1,0:T(8,128)(2,1)} %get-tuple-element.56.refs_15_), channel_id=1, source_target_pairs={{1,0},{2,1},{3,2},{4,5},{5,6},{6,7},{9,8},{10,9},{11,10},{12,13},{... | collective-permute-start | bytes 3145736 | tf_op jit(solution)/shard_map/ppermute | solution.py:278
  (12 other events, 18.5 us)

commit v3 on v2

--- a/solution.py
+++ b/solution.py
@@ -26,10 +26,55 @@
     return jnp.where(mirrored == 1, n - 1 - me, me)
 
 
+def scale_kernel(weight_ref, gain_ref, out_ref, gain_row, held, scaled, sems):
+    rows, width = held.shape
+    block = rows // sems.shape[0]
+
+    def copy(j, k):
+        some = pl.ds(j * block, block)
+        source, target = ((weight_ref, held), (scaled, out_ref))[k]
+        return pltpu.make_async_copy(source.at[some], target.at[some], sems.at[j, k])
+
+    gain_in = pltpu.make_async_copy(gain_ref, gain_row, sems.at[0, 2])
+    gain_in.start()
+    for j in range(rows // block):
+        copy(j, 0).start()
+    gain_in.wait()
+    gain = jnp.broadcast_to(gain_row[:, :rows].astype(f32), (128, rows)).T
+    for j in range(rows // block):
+        some = slice(j * block, (j + 1) * block)
+        copy(j, 0).wait()
+        for start in range(0, width, 128):
+            lanes = slice(start, start + 128)
+            scaled[some, lanes] = (held[some, lanes].astype(f32) * gain[some]).astype(bf16)
+        copy(j, 1).start()
+    for j in range(rows // block):
+        copy(j, 1).wait()
+
+
+def scale_first(weight, gain, rows):
+    key_width = weight.shape[1]
+    any_spec = pl.BlockSpec(memory_space=pl.ANY)
+    return pl.pallas_call(
+        scale_kernel,
+        out_shape=jax.ShapeDtypeStruct((rows, key_width), bf16),
+        in_specs=[any_spec, any_spec],
+        out_specs=any_spec,
+        scratch_shapes=[
+            pltpu.VMEM(gain.shape, bf16),
+            pltpu.VMEM((rows, key_width), bf16),
+            pltpu.VMEM((rows, key_width), bf16),
+            pltpu.SemaphoreType.DMA((4, 3)),
+        ],
+        compiler_params=pltpu.CompilerParams(vmem_limit_bytes=56 * 2**20),
+        cost_estimate=pl.CostEstimate(flops=0, bytes_accessed=2 * 2**20, transcendentals=0),
+    )(weight, gain)
+
+
 def pass_on_kernel(n, s, c, inputs, split, me_ref, x_ref, c_ref, *refs):
     there, back = refs[0], refs[1]
     outs = refs[inputs:]
-    columns, held, sems = refs[-3:]
+    cotangent, columns, held, sems = refs[-4:]
     me, mirrored = me_ref[0], me_ref[1]
     rows, block = held.shape[1], columns.shape[3]
     steps = rows // block
@@ -51,16 +96,21 @@
         target = outs[d * split + j * block // part].at[pl.ds(j * block % part, block)]
         return pltpu.make_async_copy(held.at[d, some(j)], target, sems.at[d, j, 2])
 
+    def cotangent_in(d):
+        return pltpu.make_async_copy(c_ref, cotangent.at[d], sems.at[d, 0, 3])
+
     def fetch(d):
+        cotangent_in(d).start()
         for j in range(steps):
             columns_in(d, j).start()
             sum_in(d, j).start()
 
     def add(d):
+        cotangent_in(d).wait()
         for j in range(steps):
             columns_in(d, j).wait()
             sum_in(d, j).wait()
-            term = dot(columns[d, j], c_ref[...], CONTRACT_ROWS)
+            term = dot(columns[d, j], cotangent[d], CONTRACT_ROWS)
             held[d, some(j)] = (held[d, some(j)].astype(f32) + term).astype(bf16)
             sum_out(d, j).start()
 
@@ -92,14 +142,15 @@
         in_specs=[
             pl.BlockSpec(memory_space=pltpu.SMEM),
             any_spec,
-            pl.BlockSpec(memory_space=pltpu.VMEM),
+            any_spec,
         ]
         + [any_spec] * len(operands),
         out_specs=[any_spec] * len(outs),
         scratch_shapes=[
+            pltpu.VMEM((2, tokens_here, key_width), bf16),
             pltpu.VMEM((2, rows // block, tokens_here, block), bf16),
             pltpu.VMEM((2, rows, key_width), bf16),
-            pltpu.SemaphoreType.DMA((2, rows // block, 3)),
+            pltpu.SemaphoreType.DMA((2, rows // block, 4)),
         ],
         input_output_aliases=aliases,
         compiler_params=pltpu.CompilerParams(vmem_limit_bytes=56 * 2**20),
@@ -200,41 +251,51 @@
     )(me, activations, key_cotangent, inverse, *pieces)
 
 
-def weight_kernel(factor, first, x_ref, c_ref, right_ref, left_ref, weight_ref, gain_ref, *refs):
-    grad_ref, gain_grad_ref, grad, gain_grad, sems = refs[-5:]
+def weight_kernel(factor, first, own_ref, right_ref, left_ref, weight_ref, gain_ref, *refs):
+    grad_ref, gain_grad_ref, right, left, grad, gain_grad, sems = refs[-7:]
     rows, width = grad.shape
-    block = 256
+    block = rows // (sems.shape[0] - 1)
+    steps = rows // block
+
+    def copy(j, k):
+        some, mine = slice(j * block, (j + 1) * block), slice(first + j * block, first + (j + 1) * block)
+        source = (right_ref, left_ref, grad)[k].at[some]
+        target = grad_ref.at[mine] if k == 2 else (right, left)[k].at[some]
+        return pltpu.make_async_copy(source, target, sems.at[j, k])
+
+    for j in range(steps):
+        copy(j, 0).start()
+        copy(j, 1).start()
     gain = jnp.broadcast_to(gain_ref[:, first : first + rows].astype(f32) * factor, (128, rows)).T
-    copies = []
-    for j in range(0, rows, block):
-        some, mine = slice(j, j + block), slice(first + j, first + j + block)
-        own = dot(x_ref[:, mine], c_ref[...], CONTRACT_ROWS)
+    for j in range(steps):
+        some, mine = slice(j * block, (j + 1) * block), slice(first + j * block, first + (j + 1) * block)
+        copy(j, 0).wait()
+        copy(j, 1).wait()
         folded = None
         for start in range(0, width, 128):
             lanes = slice(start, start + 128)
-            summed = own[:, lanes] + right_ref[some, lanes].astype(f32) + left_ref[some, lanes].astype(f32)
+            summed = right[some, lanes].astype(f32) + left[some, lanes].astype(f32)
+            summed = own_ref[some, lanes] + summed
             grad[some, lanes] = (summed * gain[some]).astype(bf16)
             terms = summed * weight_ref[mine, lanes].astype(f32)
             folded = terms if folded is None else folded + terms
-        copies.append(pltpu.make_async_copy(grad.at[some], grad_ref.at[mine], sems.at[j // block]))
-        copies[-1].start()
+        copy(j, 2).start()
         gain_grad[:, some] = jnp.sum(folded.T, axis=0, keepdims=True) * factor
-    copies.append(
-        pltpu.make_async_copy(
-            gain_grad, gain_grad_ref.at[:, first : first + rows], sems.at[rows // block]
-        )
-    )
-    copies[-1].start()
-    for copy in copies:
-        copy.wait()
-
-
-def weight_piece(factor, first, columns, cotangent, right, left, weight, gain, so_far):
+    there = gain_grad_ref.at[:, first : first + rows]
+    gain_out = pltpu.make_async_copy(gain_grad, there, sems.at[steps, 0])
+    gain_out.start()
+    for j in range(steps):
+        copy(j, 2).wait()
+    gain_out.wait()
+
+
+def weight_piece(factor, first, own, right, left, weight, gain, so_far):
     shard, key_width = weight.shape
     rows = right.shape[0]
     any_spec = pl.BlockSpec(memory_space=pl.ANY)
-    operands = [columns, cotangent, right, left, weight, gain]
-    in_specs = [pl.BlockSpec(memory_space=pltpu.VMEM)] * len(operands)
+    operands = [own, right, left, weight, gain]
+    vmem = pl.BlockSpec(memory_space=pltpu.VMEM)
+    in_specs = [vmem, any_spec, any_spec, vmem, vmem]
     aliases = {}
     if so_far is not None:
         aliases = {len(operands): 0, len(operands) + 1: 1}
@@ -250,8 +311,10 @@
         out_specs=(any_spec, any_spec),
         scratch_shapes=[
             pltpu.VMEM((rows, key_width), bf16),
+            pltpu.VMEM((rows, key_width), bf16),
+            pltpu.VMEM((rows, key_width), bf16),
             pltpu.VMEM((1, rows), f32),
-            pltpu.SemaphoreType.DMA((rows // 256 + 1,)),
+            pltpu.SemaphoreType.DMA((rows // 256 + 1, 3)),
         ],
         input_output_aliases=aliases,
         compiler_params=pltpu.CompilerParams(vmem_limit_bytes=16 * 2**20),
@@ -284,7 +347,7 @@
         part = slice(c * rows, (c + 1) * rows)
         return (weight[part].astype(f32) * gain[part]).astype(bf16)
 
-    first = scaled(weight, 0)
+    first = scale_first(weight, norm_gain, rows)
     first, weight, activations = lax.optimization_barrier((first, weight, activations))
     own, flying = [first], [send(first, first)]
 
@@ -317,15 +380,18 @@
             tokens, rider = list(before), None
             if (s, c) == (1, 1):
                 total = jnp.sum(delta, axis=0)
+            if (s, c) == (2, 1):
+                total = total + swapped
             if (s, c) in ((1, 1), (2, 1)):
                 rider = total
             if (s, c) == (2, 0):
-                tokens.append(total)
+                tokens.append(swapped)
             outs = pass_on(
                 s, c, n, where_am_i, activations, cotangent, there, back, tokens, rider, split
             )
             if (s, c) == (1, 1):
-                total = outs[-1] + lax.ppermute(outs[-1], "zh", [(0, 1), (1, 0)])
+                swapped = lax.ppermute(outs[-1], "zh", [(0, 1), (1, 0)])
+                total = outs[-1]
             if (s, c) == (2, 1):
                 delta = jnp.broadcast_to(outs[-1][None], spread)
                 delta = lax.all_to_all(delta, plane, 0, 0, tiled=True)
@@ -347,13 +413,12 @@
     new_momentum = momentum_decay * outer_momentum + increment
     new_params = outer_params - outer_rate * (increment + momentum_decay * new_momentum)
 
-    columns = lax.dynamic_slice_in_dim(activations, lax.axis_index("fsdp") * shard, shard, 1)
-    so_far, start = None, 0
-    for right, left in flying:
-        so_far = weight_piece(
-            factor, start, columns, cotangent, right, left, weight, norm_gain, so_far
-        )
-        start += right.shape[0]
+    so_far = None
+    for c, (right, left) in enumerate(flying):
+        start = lax.axis_index("fsdp") * shard + c * rows
+        columns = lax.dynamic_slice_in_dim(activations, start, rows, 1)
+        term = dot(columns, cotangent, CONTRACT_ROWS)
+        so_far = weight_piece(factor, c * rows, term, right, left, weight, norm_gain, so_far)
     weight_grad, gain_grad = so_far
     return (keys, input_grad, weight_grad[None], gain_grad, new_params, new_momentum)
 

time: 196 us -> 195 us (level)
  waiting for transfers between devices: 42.5 us -> 34.5 us
  matrix products: 0 us -> 5.79 us
  local copies, waits for them, and re-layouts: 12.3 us -> 15.6 us
  other arithmetic: 17.2 us -> 14.6 us
    ppermute x16, waiting for transfers between devices: 22.5 us -> 14.1 us  [send(): return [lax.ppermute(there, line, up), lax.ppermute(back, line, down)]]
    unnamed x34 -> x48, local copies, waits for them, and re-layouts: 7.29 us -> 13.6 us
    dot_general x0 -> x2, matrix products: none -> 5.79 us  [dot(): return lax.dot_general(a, b, dims, preferred_element_type=f32)]
    convert_element_type x2 -> x1, other arithmetic: 3.74 us -> 1.26 us  [scaled(): return (weight[part].astype(f32) * gain[part]).astype(bf16)]
    dynamic_slice x1 -> x0, local copies, waits for them, and re-layouts: 2.34 us -> none  [body(): lax.dynamic_slice_in_dim(activations, lax.axis_index('fsdp') * shard, sha...]
    pallas_call x0 -> x1, Pallas kernels: none -> 2.09 us  [scale_first(): pl.pallas_call(scale_kernel, out_shape=jax.ShapeDtypeStruct((rows, key_wi...]
  transfers between devices with their start and end apart: 19 -> 19, of which waited for: 8 -> 7; matrix products, arithmetic and copies ran while one was open for 10% -> 12% of each run, Pallas kernels for 20% -> 19%
where the time goes in v3:
time: 195 us; the launch traced here: 193 us
  starting transfers between devices  79.3 us (41%)
  Pallas kernels  41.4 us (21%)
  waiting for transfers between devices  34.5 us (18%)
  local copies, waits for them, and re-layouts  15.6 us (8%)
  other arithmetic  14.6 us (7%)
  matrix products  5.79 us (3%)
    ppermute x16, starting transfers between devices, send(): return [lax.ppermute(there, line, up), lax.ppermute(back, line, down)]  54.8 us
    pallas_call x6, Pallas kernels, pass_on(): pl.pallas_call(functools.partial(pass_on_kernel, n, s, c, len(operands),...  23.1 us
    all_to_all x2, starting transfers between devices, body(): delta = lax.all_to_all(delta, plane, 0, 0, tiled=True)  17.6 us
    ppermute x1, waiting for transfers between devices, body(): swapped = lax.ppermute(outs[-1], 'zh', [(0, 1), (1, 0)])  15 us
    ppermute x16, waiting for transfers between devices, send(): return [lax.ppermute(there, line, up), lax.ppermute(back, line, down)]  14.1 us
    unnamed x48, local copies, waits for them, and re-layouts  13.6 us
    pallas_call x1, Pallas kernels, project(): pl.pallas_call(functools.partial(project_kernel, n, factor, len(waits)),...  10.7 us
    ppermute x1, starting transfers between devices, body(): swapped = lax.ppermute(outs[-1], 'zh', [(0, 1), (1, 0)])  6.92 us
  transfers between devices with their start and end apart: 19, of which 7 were waited for; matrix products, arithmetic and copies ran while one was open for 12% of the time, Pallas kernels for 19%

profile of v3, /device:TPU:1, one launch (start us, length us, event | category | flops | bytes accessed | tf_op | source)
XLA Modules:
  0.0 193.1 jit_solution(11619000807541727784)
XLA Ops:
  4.0 6.0 %collective-permute-start.1 = (bf16[1024,512]{1,0:T(8,128)(2,1)}, bf16[1024,512]{1,0:T(8,128)(2,1)}, u32[]{:S(2)}, u32[]{:S(2)}) collective-permute-start(bf16[1024,512]{1,0:T(8,128)(2,1)} %shard_map.118.refs_0_), channel_id=1, source_target_pairs={{1,0},{2,1},{3,2},{4,5},{5,6},{6,7},{9,8},{10,9},{11,10},{12,13},{... | collective-permute-start | bytes 3145736 | tf_op jit(solution)/shard_map/ppermute | solution.py:341
  10.7 3.3 %multiply_reduce_fusion = f32[256]{0:T(256)S(1)} fusion(bf16[256,8192]{1,0:T(8,128)(2,1)} %x_ref.6), kind=kLoop, calls=%fused_computation | loop fusion | flops 6291200 | bytes 4195328 | tf_op jit(solution)/shard_map/reduce_sum | solution.py:362
  19.7 5.0 %collective-permute-start.3 = (bf16[1024,512]{1,0:T(8,128)(2,1)}, bf16[1024,512]{1,0:T(8,128)(2,1)}, u32[]{:S(2)}, u32[]{:S(2)}) collective-permute-start(bf16[1024,512]{1,0:T(8,128)(2,1)} %multiply_convert_fusion.refs_1_), channel_id=1, source_target_pairs={{1,0},{2,1},{3,2},{4,5},{5,6},{6,7},{9,8},{10,9},{11,10},{12,13},{... | collective-permute-start | bytes 3145736 | tf_op jit(solution)/shard_map/ppermute | solution.py:341
  24.7 7.3 %all-to-all-start = ((f32[32,64,128]{2,1,0:T(8,128)}), f32[32,64,128]{2,1,0:T(8,128)}, u32[]{:S(2)}, u32[]{:S(2)}) async-start(f32[32,64,128]{2,1,0:T(8,128)} %bitcast.26), calls=%async_computation | async-start | bytes 2097152 | tf_op jit(solution)/shard_map/all_to_all | solution.py:370
  33.5 3.8 %shard_map.119 = (bf16[1024,512]{1,0:T(8,128)(2,1)}, bf16[1024,512]{1,0:T(8,128)(2,1)}) custom-call(s32[2]{0:T(128)} %pad_add_fusion.me_ref, bf16[256,8192]{1,0:T(8,128)(2,1)} %x_ref.6, bf16[256,512]{1,0:T(8,128)(2,1)} %multiply_convert_fusion.1.c_ref, bf16[1024,512]{1,0:T(8,128)(2,1)} %copy-done.6, ...), custom_call_target="tpu_custom_call", output_to_operand_aliasing={{0}: (3, {}), {1}: (4, {})} | custom-call | bytes 4194304 | tf_op jit(solution)/shard_map/pallas_call | solution.py:139
  38.6 5.0 %collective-permute-start.5 = (bf16[1024,512]{1,0:T(8,128)(2,1)}, bf16[1024,512]{1,0:T(8,128)(2,1)}, u32[]{:S(2)}, u32[]{:S(2)}) collective-permute-start(bf16[1024,512]{1,0:T(8,128)(2,1)} %get-tuple-element.45.refs_4_.refs_8_), channel_id=1, source_target_pairs={{1,0},{2,1},{3,2},{4,5},{5,6},{6,7},{9,8},{10,9},{11,10},{12,13},{... | collective-permute-start | bytes 3145736 | tf_op jit(solution)/shard_map/ppermute | solution.py:341
  43.6 5.4 %all-to-all-done = f32[32,64,128]{2,1,0:T(8,128)} async-done(((f32[32,64,128]{2,1,0:T(8,128)}), f32[32,64,128]{2,1,0:T(8,128)}, u32[]{:S(2)}, u32[]{:S(2)}) %all-to-all-start) | async-done | bytes 1048608 | tf_op jit(solution)/shard_map/all_to_all | solution.py:370
  50.9 3.9 %collective-permute-done.3.refs_1_ = bf16[1024,512]{1,0:T(8,128)(2,1)} collective-permute-done((bf16[1024,512]{1,0:T(8,128)(2,1)}, bf16[1024,512]{1,0:T(8,128)(2,1)}, u32[]{:S(2)}, u32[]{:S(2)}) %collective-permute-start.3) | collective-permute-done | bytes 1048608 | tf_op jit(solution)/shard_map/ppermute | solution.py:341
  54.7 3.8 %shard_map.120 = (bf16[1024,512]{1,0:T(8,128)(2,1)}, bf16[1024,512]{1,0:T(8,128)(2,1)}, f32[64,128]{1,0:T(8,128)}) custom-call(s32[2]{0:T(128)} %pad_add_fusion.me_ref, bf16[256,8192]{1,0:T(8,128)(2,1)} %x_ref.6, bf16[256,512]{1,0:T(8,128)(2,1)} %multiply_convert_fusion.1.c_ref, ...), custom_call_target="tpu_custom_call", output_to_operand_aliasing={{0}: (3, {}), {1}: (4, {}), {2}: (5, {})} | custom-call | bytes 4194304 | tf_op jit(solution)/shard_map/pallas_call | solution.py:139
  58.5 6.9 %collective-permute-start.6 = (f32[64,128]{1,0:T(8,128)}, f32[64,128]{1,0:T(8,128)S(1)}, u32[]{:S(2)}, u32[]{:S(2)}) collective-permute-start(f32[64,128]{1,0:T(8,128)} %get-tuple-element.48), channel_id=1, source_target_pairs={{0,8},{8,0},{1,9},{9,1},{2,10},{10,2},{3,11},{11,3},{4,12},{12,4},... | collective-permute-start | bytes 98312 | tf_op jit(solution)/shard_map/ppermute | solution.py:393
  66.7 4.1 %collective-permute-start.8 = (bf16[1024,512]{1,0:T(8,128)(2,1)}, bf16[1024,512]{1,0:T(8,128)(2,1)S(1)}, u32[]{:S(2)}, u32[]{:S(2)}) collective-permute-start(bf16[1024,512]{1,0:T(8,128)(2,1)} %get-tuple-element.47.refs_3_.refs_9_), channel_id=1, source_target_pairs={{1,0},{2,1},{3,2},{4,5},{5,6},{6,7},{9,8},{10,9},{11,10},{12,13},{... | collective-permute-start | bytes 3145736 | tf_op jit(solution)/shard_map/ppermute | solution.py:341
  70.8 15.0 %collective-permute-done.6.refs_4_ = f32[64,128]{1,0:T(8,128)S(1)} collective-permute-done((f32[64,128]{1,0:T(8,128)}, f32[64,128]{1,0:T(8,128)S(1)}, u32[]{:S(2)}, u32[]{:S(2)}) %collective-permute-start.6) | collective-permute-done | bytes 32800 | tf_op jit(solution)/shard_map/ppermute | solution.py:393
  88.2 3.8 %shard_map.121 = (bf16[1024,512]{1,0:T(8,128)(2,1)}, bf16[1024,512]{1,0:T(8,128)(2,1)}) custom-call(s32[2]{0:T(128)} %pad_add_fusion.me_ref, bf16[256,8192]{1,0:T(8,128)(2,1)} %x_ref.6, bf16[256,512]{1,0:T(8,128)(2,1)} %multiply_convert_fusion.1.c_ref, bf16[1024,512]{1,0:T(8,128)(2,1)} %copy-done.13, ...), custom_call_target="tpu_custom_call", output_to_operand_aliasing={{0}: (3, {}), {1}: (4, {})} | custom-call | flops 99999997952 | bytes 4194304 | tf_op jit(solution)/shard_map/pallas_call | solution.py:139
  93.2 5.0 %collective-permute-start.11 = (bf16[1024,512]{1,0:T(8,128)(2,1)}, bf16[1024,512]{1,0:T(8,128)(2,1)}, u32[]{:S(2)}, u32[]{:S(2)}) collective-permute-start(bf16[1024,512]{1,0:T(8,128)(2,1)} %get-tuple-element.50.refs_4_.refs_10_), channel_id=1, source_target_pairs={{1,0},{2,1},{3,2},{4,5},{5,6},{6,7},{9,8},{10,9},{11,10},{12,13},{... | collective-permute-start | bytes 3145736 | tf_op jit(solution)/shard_map/ppermute | solution.py:341
  102.1 3.8 %shard_map.122 = (bf16[1024,512]{1,0:T(8,128)(2,1)}, bf16[1024,512]{1,0:T(8,128)(2,1)}, f32[64,128]{1,0:T(8,128)}) custom-call(s32[2]{0:T(128)} %pad_add_fusion.me_ref, bf16[256,8192]{1,0:T(8,128)(2,1)} %x_ref.6, bf16[256,512]{1,0:T(8,128)(2,1)} %multiply_convert_fusion.1.c_ref, ...), custom_call_target="tpu_custom_call", output_to_operand_aliasing={{0}: (3, {}), {1}: (4, {}), {2}: (5, {})} | custom-call | bytes 4194304 | tf_op jit(solution)/shard_map/pallas_call | solution.py:139
  107.1 5.6 %collective-permute-start.12 = (bf16[1024,512]{1,0:T(8,128)(2,1)}, bf16[1024,512]{1,0:T(8,128)(2,1)}, u32[]{:S(2)}, u32[]{:S(2)}) collective-permute-start(bf16[1024,512]{1,0:T(8,128)(2,1)} %get-tuple-element.52.refs_3_.refs_11_), channel_id=1, source_target_pairs={{1,0},{2,1},{3,2},{4,5},{5,6},{6,7},{9,8},{10,9},{11,10},{12,13},{... | collective-permute-start | bytes 3145736 | tf_op jit(solution)/shard_map/ppermute | solution.py:341
  114.6 10.3 %all-to-all-start.1 = ((f32[32,64,128]{2,1,0:T(8,128)}), f32[32,64,128]{2,1,0:T(8,128)}, u32[]{:S(2)}, u32[]{:S(2)}) async-start(f32[32,64,128]{2,1,0:T(8,128)} %broadcast_in_dim.4), calls=%async_computation.1 | async-start | bytes 2097152 | tf_op jit(solution)/shard_map/all_to_all | solution.py:397
  125.1 3.0 %fusion.4.own_ref = f32[1024,512]{1,0:T(8,128)} fusion(bf16[256,512]{1,0:T(8,128)(2,1)} %multiply_convert_fusion.1.c_ref, bf16[256,8192]{1,0:T(8,128)(2,1)} %x_ref.6, s32[]{:T(128)S(6)} %select_n.22), kind=kOutput, calls=%fused_computation.10 | convolution fusion | flops 268435456 | bytes 2883588 | tf_op jit(solution)/shard_map/dot_general | solution.py:22
  131.9 3.8 %shard_map.123 = (bf16[1024,512]{1,0:T(8,128)(2,1)}, bf16[1024,512]{1,0:T(8,128)(2,1)}) custom-call(s32[2]{0:T(128)} %pad_add_fusion.me_ref, bf16[256,8192]{1,0:T(8,128)(2,1)} %x_ref.6, bf16[256,512]{1,0:T(8,128)(2,1)} %multiply_convert_fusion.1.c_ref, bf16[1024,512]{1,0:T(8,128)(2,1)} %copy-done.11, ...), custom_call_target="tpu_custom_call" | custom-call | bytes 4194304 | tf_op jit(solution)/shard_map/pallas_call | solution.py:139
  137.0 7.2 %collective-permute-start.16 = (bf16[1024,512]{1,0:T(8,128)(2,1)}, bf16[1024,512]{1,0:T(8,128)(2,1)}, u32[]{:S(2)}, u32[]{:S(2)}) collective-permute-start(bf16[1024,512]{1,0:T(8,128)(2,1)} %get-tuple-element.54.refs_3_), channel_id=1, source_target_pairs={{1,0},{2,1},{3,2},{4,5},{5,6},{6,7},{9,8},{10,9},{11,10},{12,13},{... | collective-permute-start | bytes 3145736 | tf_op jit(solution)/shard_map/ppermute | solution.py:341
  146.0 4.3 %shard_map.124 = (bf16[1024,512]{1,0:T(8,128)(2,1)}, bf16[1024,512]{1,0:T(8,128)(2,1)}) custom-call(s32[2]{0:T(128)} %pad_add_fusion.me_ref, bf16[256,8192]{1,0:T(8,128)(2,1)} %x_ref.6, bf16[256,512]{1,0:T(8,128)(2,1)} %multiply_convert_fusion.1.c_ref, bf16[1024,512]{1,0:T(8,128)(2,1)} %collective-permute-done.10.refs_0_.refs_7_, ...), custom_call_target="tpu_custom_call" | custom-call | bytes 4194304 | tf_op jit(solution)/shard_map/pallas_call | solution.py:139
  151.6 6.7 %collective-permute-start.14 = (bf16[1024,512]{1,0:T(8,128)(2,1)}, bf16[1024,512]{1,0:T(8,128)(2,1)}, u32[]{:S(2)}, u32[]{:S(2)}) collective-permute-start(bf16[1024,512]{1,0:T(8,128)(2,1)} %get-tuple-element.56.refs_15_), channel_id=1, source_target_pairs={{1,0},{2,1},{3,2},{4,5},{5,6},{6,7},{9,8},{10,9},{11,10},{12,13},{... | collective-permute-start | bytes 3145736 | tf_op jit(solution)/shard_map/ppermute | solution.py:341
  166.9 10.7 %shard_map.125 = (bf16[256,512]{1,0:T(8,128)(2,1)}, bf16[256,8192]{1,0:T(8,128)(2,1)}) custom-call(s32[2]{0:T(128)S(1)} %copy-done.19, bf16[256,8192]{1,0:T(8,128)(2,1)S(1)} %copy-done, bf16[256,512]{1,0:T(8,128)(2,1)S(1)} %copy-done.15, f32[256,1]{1,0:T(8,128)S(1)} %copy.25.inverse_ref, bf16[1024,512]{1,0:T(8,128)(2,1)S(1)} %copy-done.10, ...), custom_call_target="tpu_custom_call" | custom-call | flops 4294967296 | bytes 16777216 | tf_op jit(solution)/shard_map/pallas_call | solution.py:230
  186.6 3.6 %collective-permute-done.14.left_ref = bf16[1024,512]{1,0:T(8,128)(2,1)} collective-permute-done((bf16[1024,512]{1,0:T(8,128)(2,1)}, bf16[1024,512]{1,0:T(8,128)(2,1)}, u32[]{:S(2)}, u32[]{:S(2)}) %collective-permute-start.14) | collective-permute-done | bytes 1048608 | tf_op jit(solution)/shard_map/ppermute | solution.py:341
  (87 shorter events, 54.3 us)
Async XLA Ops:
  2.7 29.8 %collective-permute-start = (bf16[1024,512]{1,0:T(8,128)(2,1)}, bf16[1024,512]{1,0:T(8,128)(2,1)S(1)}, u32[]{:S(2)}, u32[]{:S(2)}) collective-permute-start(bf16[1024,512]{1,0:T(8,128)(2,1)} %shard_map.118.refs_0_), channel_id=1, source_target_pairs={{0,1},{1,2},{2,3},{5,4},{6,5},{7,6},{8,9},{9,10},{10,11},{13,12},{... | collective-permute-start | bytes 3145736 | tf_op jit(solution)/shard_map/ppermute | solution.py:341
  4.0 28.6 %collective-permute-start.1 = (bf16[1024,512]{1,0:T(8,128)(2,1)}, bf16[1024,512]{1,0:T(8,128)(2,1)}, u32[]{:S(2)}, u32[]{:S(2)}) collective-permute-start(bf16[1024,512]{1,0:T(8,128)(2,1)} %shard_map.118.refs_0_), channel_id=1, source_target_pairs={{1,0},{2,1},{3,2},{4,5},{5,6},{6,7},{9,8},{10,9},{11,10},{12,13},{... | collective-permute-start | bytes 3145736 | tf_op jit(solution)/shard_map/ppermute | solution.py:341
  10.7 4.1 %copy-start.1 = (bf16[1,2048,512]{2,1,0:T(8,128)(2,1)S(1)}, bf16[1,2048,512]{2,1,0:T(8,128)(2,1)}, u32[]{:S(2)}) copy-start(bf16[1,2048,512]{2,1,0:T(8,128)(2,1)} %param.9) | copy-start | bytes 6291460
  18.4 32.4 %collective-permute-start.2 = (bf16[1024,512]{1,0:T(8,128)(2,1)}, bf16[1024,512]{1,0:T(8,128)(2,1)}, u32[]{:S(2)}, u32[]{:S(2)}) collective-permute-start(bf16[1024,512]{1,0:T(8,128)(2,1)} %multiply_convert_fusion.refs_1_), channel_id=1, source_target_pairs={{0,1},{1,2},{2,3},{5,4},{6,5},{7,6},{8,9},{9,10},{10,11},{13,12},{... | collective-permute-start | bytes 3145736 | tf_op jit(solution)/shard_map/ppermute | solution.py:341
  19.7 35.0 %collective-permute-start.3 = (bf16[1024,512]{1,0:T(8,128)(2,1)}, bf16[1024,512]{1,0:T(8,128)(2,1)}, u32[]{:S(2)}, u32[]{:S(2)}) collective-permute-start(bf16[1024,512]{1,0:T(8,128)(2,1)} %multiply_convert_fusion.refs_1_), channel_id=1, source_target_pairs={{1,0},{2,1},{3,2},{4,5},{5,6},{6,7},{9,8},{10,9},{11,10},{12,13},{... | collective-permute-start | bytes 3145736 | tf_op jit(solution)/shard_map/ppermute | solution.py:341
  24.7 24.2 %all-to-all-start = ((f32[32,64,128]{2,1,0:T(8,128)}), f32[32,64,128]{2,1,0:T(8,128)}, u32[]{:S(2)}, u32[]{:S(2)}) async-start(f32[32,64,128]{2,1,0:T(8,128)} %bitcast.26), calls=%async_computation | async-start | bytes 2097152 | tf_op jit(solution)/shard_map/all_to_all | solution.py:370
  37.3 49.9 %collective-permute-start.4 = (bf16[1024,512]{1,0:T(8,128)(2,1)}, bf16[1024,512]{1,0:T(8,128)(2,1)S(1)}, u32[]{:S(2)}, u32[]{:S(2)}) collective-permute-start(bf16[1024,512]{1,0:T(8,128)(2,1)} %get-tuple-element.43.refs_3_.refs_2_), channel_id=1, source_target_pairs={{0,1},{1,2},{2,3},{5,4},{6,5},{7,6},{8,9},{9,10},{10,11},{13,12},{... | collective-permute-start | bytes 3145736 | tf_op jit(solution)/shard_map/ppermute | solution.py:341
  38.6 48.6 %collective-permute-start.5 = (bf16[1024,512]{1,0:T(8,128)(2,1)}, bf16[1024,512]{1,0:T(8,128)(2,1)}, u32[]{:S(2)}, u32[]{:S(2)}) collective-permute-start(bf16[1024,512]{1,0:T(8,128)(2,1)} %get-tuple-element.45.refs_4_.refs_8_), channel_id=1, source_target_pairs={{1,0},{2,1},{3,2},{4,5},{5,6},{6,7},{9,8},{10,9},{11,10},{12,13},{... | collective-permute-start | bytes 3145736 | tf_op jit(solution)/shard_map/ppermute | solution.py:341
  58.5 27.2 %collective-permute-start.6 = (f32[64,128]{1,0:T(8,128)}, f32[64,128]{1,0:T(8,128)S(1)}, u32[]{:S(2)}, u32[]{:S(2)}) collective-permute-start(f32[64,128]{1,0:T(8,128)} %get-tuple-element.48), channel_id=1, source_target_pairs={{0,8},{8,0},{1,9},{9,1},{2,10},{10,2},{3,11},{11,3},{4,12},{12,4},... | collective-permute-start | bytes 98312 | tf_op jit(solution)/shard_map/ppermute | solution.py:393
  65.5 32.8 %collective-permute-start.7 = (bf16[1024,512]{1,0:T(8,128)(2,1)}, bf16[1024,512]{1,0:T(8,128)(2,1)S(1)}, u32[]{:S(2)}, u32[]{:S(2)}) collective-permute-start(bf16[1024,512]{1,0:T(8,128)(2,1)} %get-tuple-element.46.refs_2_.refs_3_), channel_id=1, source_target_pairs={{0,1},{1,2},{2,3},{5,4},{6,5},{7,6},{8,9},{9,10},{10,11},{13,12},{... | collective-permute-start | bytes 3145736 | tf_op jit(solution)/shard_map/ppermute | solution.py:341
  66.7 34.3 %collective-permute-start.8 = (bf16[1024,512]{1,0:T(8,128)(2,1)}, bf16[1024,512]{1,0:T(8,128)(2,1)S(1)}, u32[]{:S(2)}, u32[]{:S(2)}) collective-permute-start(bf16[1024,512]{1,0:T(8,128)(2,1)} %get-tuple-element.47.refs_3_.refs_9_), channel_id=1, source_target_pairs={{1,0},{2,1},{3,2},{4,5},{5,6},{6,7},{9,8},{10,9},{11,10},{12,13},{... | collective-permute-start | bytes 3145736 | tf_op jit(solution)/shard_map/ppermute | solution.py:341
  91.9 39.0 %collective-permute-start.9 = (bf16[1024,512]{1,0:T(8,128)(2,1)}, bf16[1024,512]{1,0:T(8,128)(2,1)S(1)}, u32[]{:S(2)}, u32[]{:S(2)}) collective-permute-start(bf16[1024,512]{1,0:T(8,128)(2,1)} %get-tuple-element.49.refs_3_.refs_4_), channel_id=1, source_target_pairs={{0,1},{1,2},{2,3},{5,4},{6,5},{7,6},{8,9},{9,10},{10,11},{13,12},{... | collective-permute-start | bytes 3145736 | tf_op jit(solution)/shard_map/ppermute | solution.py:341
  93.2 37.7 %collective-permute-start.11 = (bf16[1024,512]{1,0:T(8,128)(2,1)}, bf16[1024,512]{1,0:T(8,128)(2,1)}, u32[]{:S(2)}, u32[]{:S(2)}) collective-permute-start(bf16[1024,512]{1,0:T(8,128)(2,1)} %get-tuple-element.50.refs_4_.refs_10_), channel_id=1, source_target_pairs={{1,0},{2,1},{3,2},{4,5},{5,6},{6,7},{9,8},{10,9},{11,10},{12,13},{... | collective-permute-start | bytes 3145736 | tf_op jit(solution)/shard_map/ppermute | solution.py:341
  105.8 38.4 %collective-permute-start.10 = (bf16[1024,512]{1,0:T(8,128)(2,1)}, bf16[1024,512]{1,0:T(8,128)(2,1)}, u32[]{:S(2)}, u32[]{:S(2)}) collective-permute-start(bf16[1024,512]{1,0:T(8,128)(2,1)} %get-tuple-element.51.refs_2_.refs_5_), channel_id=1, source_target_pairs={{0,1},{1,2},{2,3},{5,4},{6,5},{7,6},{8,9},{9,10},{10,11},{13,12},{... | collective-permute-start | bytes 3145736 | tf_op jit(solution)/shard_map/ppermute | solution.py:341
  107.1 38.9 %collective-permute-start.12 = (bf16[1024,512]{1,0:T(8,128)(2,1)}, bf16[1024,512]{1,0:T(8,128)(2,1)}, u32[]{:S(2)}, u32[]{:S(2)}) collective-permute-start(bf16[1024,512]{1,0:T(8,128)(2,1)} %get-tuple-element.52.refs_3_.refs_11_), channel_id=1, source_target_pairs={{1,0},{2,1},{3,2},{4,5},{5,6},{6,7},{9,8},{10,9},{11,10},{12,13},{... | collective-permute-start | bytes 3145736 | tf_op jit(solution)/shard_map/ppermute | solution.py:341
  114.6 63.1 %all-to-all-start.1 = ((f32[32,64,128]{2,1,0:T(8,128)}), f32[32,64,128]{2,1,0:T(8,128)}, u32[]{:S(2)}, u32[]{:S(2)}) async-start(f32[32,64,128]{2,1,0:T(8,128)} %broadcast_in_dim.4), calls=%async_computation.1 | async-start | bytes 2097152 | tf_op jit(solution)/shard_map/all_to_all | solution.py:397
  135.7 45.5 %collective-permute-start.15 = (bf16[1024,512]{1,0:T(8,128)(2,1)}, bf16[1024,512]{1,0:T(8,128)(2,1)}, u32[]{:S(2)}, u32[]{:S(2)}) collective-permute-start(bf16[1024,512]{1,0:T(8,128)(2,1)} %get-tuple-element.53.refs_2_), channel_id=1, source_target_pairs={{0,1},{1,2},{2,3},{5,4},{6,5},{7,6},{8,9},{9,10},{10,11},{13,12},{... | collective-permute-start | bytes 3145736 | tf_op jit(solution)/shard_map/ppermute | solution.py:341
  137.0 21.4 %copy-start.3 = (bf16[1024,512]{1,0:T(8,128)(2,1)S(1)}, bf16[1024,512]{1,0:T(8,128)(2,1)}, u32[]{:S(2)}) copy-start(bf16[1024,512]{1,0:T(8,128)(2,1)} %get-tuple-element.51.refs_2_.refs_5_) | copy-start | bytes 3145732
  137.0 21.4 %copy-start.19 = (s32[2]{0:T(128)S(1)}, s32[2]{0:T(128)}, u32[]{:S(2)}) copy-start(s32[2]{0:T(128)} %pad_add_fusion.me_ref) | copy-start | bytes 28
  137.0 44.2 %collective-permute-start.16 = (bf16[1024,512]{1,0:T(8,128)(2,1)}, bf16[1024,512]{1,0:T(8,128)(2,1)}, u32[]{:S(2)}, u32[]{:S(2)}) collective-permute-start(bf16[1024,512]{1,0:T(8,128)(2,1)} %get-tuple-element.54.refs_3_), channel_id=1, source_target_pairs={{1,0},{2,1},{3,2},{4,5},{5,6},{6,7},{9,8},{10,9},{11,10},{12,13},{... | collective-permute-start | bytes 3145736 | tf_op jit(solution)/shard_map/ppermute | solution.py:341
  146.0 12.3 %copy-start = (bf16[256,8192]{1,0:T(8,128)(2,1)S(1)}, bf16[256,8192]{1,0:T(8,128)(2,1)}, u32[]{:S(2)}) copy-start(bf16[256,8192]{1,0:T(8,128)(2,1)} %x_ref.6) | copy-start | bytes 12582916
  150.3 36.2 %collective-permute-start.13 = (bf16[1024,512]{1,0:T(8,128)(2,1)}, bf16[1024,512]{1,0:T(8,128)(2,1)}, u32[]{:S(2)}, u32[]{:S(2)}) collective-permute-start(bf16[1024,512]{1,0:T(8,128)(2,1)} %get-tuple-element.55.refs_14_), channel_id=1, source_target_pairs={{0,1},{1,2},{2,3},{5,4},{6,5},{7,6},{8,9},{9,10},{10,11},{13,12},{... | collective-permute-start | bytes 3145736 | tf_op jit(solution)/shard_map/ppermute | solution.py:341
  151.6 38.6 %collective-permute-start.14 = (bf16[1024,512]{1,0:T(8,128)(2,1)}, bf16[1024,512]{1,0:T(8,128)(2,1)}, u32[]{:S(2)}, u32[]{:S(2)}) collective-permute-start(bf16[1024,512]{1,0:T(8,128)(2,1)} %get-tuple-element.56.refs_15_), channel_id=1, source_target_pairs={{1,0},{2,1},{3,2},{4,5},{5,6},{6,7},{9,8},{10,9},{11,10},{12,13},{... | collective-permute-start | bytes 3145736 | tf_op jit(solution)/shard_map/ppermute | solution.py:341
  181.2 9.0 %copy-start.9 = (f32[1024,512]{1,0:T(8,128)S(1)}, f32[1024,512]{1,0:T(8,128)}, u32[]{:S(2)}) copy-start(f32[1024,512]{1,0:T(8,128)} %fusion.4.own_ref) | copy-start | bytes 6291460
  (19 other events, 32.0 us)

commit v4 on v3

--- a/solution.py
+++ b/solution.py
@@ -242,7 +242,7 @@
             pltpu.VMEM((tokens, model_width), f32),
             pltpu.SemaphoreType.DMA((4,)),
         ],
-        compiler_params=pltpu.CompilerParams(vmem_limit_bytes=28 * 2**20),
+        compiler_params=pltpu.CompilerParams(vmem_limit_bytes=56 * 2**20),
         cost_estimate=pl.CostEstimate(
             flops=4 * tokens * model_width * key_width,
             bytes_accessed=16 * 2**20,
@@ -350,6 +350,11 @@
     first = scale_first(weight, norm_gain, rows)
     first, weight, activations = lax.optimization_barrier((first, weight, activations))
     own, flying = [first], [send(first, first)]
+    for c in range(1, PIECES):
+        piece = scaled(weight, c)
+        piece, weight, activations = lax.optimization_barrier((piece, weight, activations))
+        own.append(piece)
+        flying.append(send(piece, piece))
 
     column_start = fragment[0] % (key_width // head_size) * head_size
     local_block = lax.dynamic_slice_in_dim(weight, column_start, head_size, 1)
@@ -361,12 +366,6 @@
     xfloat = activations.astype(f32)
     inverse = lax.rsqrt(jnp.mean(xfloat * xfloat, axis=1, keepdims=True) + epsilon)
     cotangent = (key_cotangent.astype(f32) * inverse).astype(bf16)
-    weight, delta, cotangent = lax.optimization_barrier((weight, delta, cotangent))
-    for c in range(1, PIECES):
-        piece = scaled(weight, c)
-        piece, delta = lax.optimization_barrier((piece, delta))
-        own.append(piece)
-        flying.append(send(piece, piece))
     delta = lax.all_to_all(delta, plane, 0, 0, tiled=True)
 
     from_near, from_far, last_parts = [], [], []
@@ -380,9 +379,7 @@
             tokens, rider = list(before), None
             if (s, c) == (1, 1):
                 total = jnp.sum(delta, axis=0)
-            if (s, c) == (2, 1):
-                total = total + swapped
-            if (s, c) in ((1, 1), (2, 1)):
+            if (s, c) in ((1, 1), (2, 0), (2, 1)):
                 rider = total
             if (s, c) == (2, 0):
                 tokens.append(swapped)
@@ -392,6 +389,8 @@
             if (s, c) == (1, 1):
                 swapped = lax.ppermute(outs[-1], "zh", [(0, 1), (1, 0)])
                 total = outs[-1]
+            if (s, c) == (2, 0):
+                total = outs[-1] + swapped
             if (s, c) == (2, 1):
                 delta = jnp.broadcast_to(outs[-1][None], spread)
                 delta = lax.all_to_all(delta, plane, 0, 0, tiled=True)

time: 195 us -> 195 us (level)
  local copies, waits for them, and re-layouts: 15.6 us -> 7.81 us
  waiting for transfers between devices: 34.5 us -> 41 us
  Pallas kernels: 41.4 us -> 43.4 us
    ppermute x16, waiting for transfers between devices: 14.1 us -> 24.6 us  [send(): return [lax.ppermute(there, line, up), lax.ppermute(back, line, down)]]
    unnamed x48 -> x28, local copies, waits for them, and re-layouts: 13.6 us -> 5.13 us
    all_to_all x2, waiting for transfers between devices: 5.37 us -> 1.36 us  [body(): delta = lax.all_to_all(delta, plane, 0, 0, tiled=True)]
    pallas_call x1, Pallas kernels: 10.7 us -> 13 us  [project(): pl.pallas_call(functools.partial(project_kernel, n, factor, len(waits)),...]
  transfers between devices with their start and end apart: 19 -> 19, of which waited for: 7 -> 8; matrix products, arithmetic and copies ran while one was open for 12% -> 12% of each run, Pallas kernels for 19% -> 20%
where the time goes in v4:
time: 195 us; the launch traced here: 193 us
  starting transfers between devices  79.3 us (41%)
  Pallas kernels  43.4 us (22%)
  waiting for transfers between devices  41 us (21%)
  other arithmetic  14.5 us (7%)
  local copies, waits for them, and re-layouts  7.81 us (4%)
  matrix products  5.7 us (3%)
    ppermute x16, starting transfers between devices, send(): return [lax.ppermute(there, line, up), lax.ppermute(back, line, down)]  54.7 us
    ppermute x16, waiting for transfers between devices, send(): return [lax.ppermute(there, line, up), lax.ppermute(back, line, down)]  24.6 us
    pallas_call x6, Pallas kernels, pass_on(): pl.pallas_call(functools.partial(pass_on_kernel, n, s, c, len(operands),...  22.6 us
    all_to_all x2, starting transfers between devices, body(): delta = lax.all_to_all(delta, plane, 0, 0, tiled=True)  17.6 us
    ppermute x1, waiting for transfers between devices, body(): swapped = lax.ppermute(outs[-1], 'zh', [(0, 1), (1, 0)])  15 us
    pallas_call x1, Pallas kernels, project(): pl.pallas_call(functools.partial(project_kernel, n, factor, len(waits)),...  13 us
    ppermute x1, starting transfers between devices, body(): swapped = lax.ppermute(outs[-1], 'zh', [(0, 1), (1, 0)])  6.92 us
    dot_general x2, matrix products, dot(): return lax.dot_general(a, b, dims, preferred_element_type=f32)  5.7 us
  transfers between devices with their start and end apart: 19, of which 8 were waited for; matrix products, arithmetic and copies ran while one was open for 12% of the time, Pallas kernels for 20%

profile of v4, /device:TPU:1, one launch (start us, length us, event | category | flops | bytes accessed | tf_op | source)
XLA Modules:
  0.0 193.3 jit_solution(9558325440893183709)
XLA Ops:
  4.2 6.0 %collective-permute-start.1 = (bf16[1024,512]{1,0:T(8,128)(2,1)}, bf16[1024,512]{1,0:T(8,128)(2,1)}, u32[]{:S(2)}, u32[]{:S(2)}) collective-permute-start(bf16[1024,512]{1,0:T(8,128)(2,1)} %shard_map.118.refs_0_), channel_id=1, source_target_pairs={{1,0},{2,1},{3,2},{4,5},{5,6},{6,7},{9,8},{10,9},{11,10},{12,13},{... | collective-permute-start | bytes 3145736 | tf_op jit(solution)/shard_map/ppermute | solution.py:341
  12.7 5.0 %collective-permute-start.3 = (bf16[1024,512]{1,0:T(8,128)(2,1)}, bf16[1024,512]{1,0:T(8,128)(2,1)}, u32[]{:S(2)}, u32[]{:S(2)}) collective-permute-start(bf16[1024,512]{1,0:T(8,128)(2,1)} %multiply_convert_fusion.refs_1_), channel_id=1, source_target_pairs={{1,0},{2,1},{3,2},{4,5},{5,6},{6,7},{9,8},{10,9},{11,10},{12,13},{... | collective-permute-start | bytes 3145736 | tf_op jit(solution)/shard_map/ppermute | solution.py:341
  20.8 7.3 %all-to-all-start = ((f32[32,64,128]{2,1,0:T(8,128)}), f32[32,64,128]{2,1,0:T(8,128)}, u32[]{:S(2)}, u32[]{:S(2)}) async-start(f32[32,64,128]{2,1,0:T(8,128)} %bitcast.26), calls=%async_computation | async-start | bytes 2097152 | tf_op jit(solution)/shard_map/all_to_all | solution.py:369
  28.0 3.1 %multiply_reduce_fusion = f32[256]{0:T(256)S(1)} fusion(bf16[256,8192]{1,0:T(8,128)(2,1)} %x_ref.6), kind=kLoop, calls=%fused_computation | loop fusion | flops 6291200 | bytes 4195328 | tf_op jit(solution)/shard_map/reduce_sum | solution.py:367
  33.6 3.8 %shard_map.119 = (bf16[1024,512]{1,0:T(8,128)(2,1)}, bf16[1024,512]{1,0:T(8,128)(2,1)}) custom-call(s32[2]{0:T(128)} %pad_add_fusion.me_ref, bf16[256,8192]{1,0:T(8,128)(2,1)} %x_ref.6, bf16[256,512]{1,0:T(8,128)(2,1)} %multiply_convert_fusion.1.c_ref, bf16[1024,512]{1,0:T(8,128)(2,1)} %copy-done.7, ...), custom_call_target="tpu_custom_call", output_to_operand_aliasing={{0}: (3, {}), {1}: (4, {})} | custom-call | bytes 4194304 | tf_op jit(solution)/shard_map/pallas_call | solution.py:139
  38.7 5.0 %collective-permute-start.5 = (bf16[1024,512]{1,0:T(8,128)(2,1)}, bf16[1024,512]{1,0:T(8,128)(2,1)}, u32[]{:S(2)}, u32[]{:S(2)}) collective-permute-start(bf16[1024,512]{1,0:T(8,128)(2,1)} %get-tuple-element.42.refs_4_.refs_8_), channel_id=1, source_target_pairs={{1,0},{2,1},{3,2},{4,5},{5,6},{6,7},{9,8},{10,9},{11,10},{12,13},{... | collective-permute-start | bytes 3145736 | tf_op jit(solution)/shard_map/ppermute | solution.py:341
  48.9 6.1 %collective-permute-done.3.refs_1_ = bf16[1024,512]{1,0:T(8,128)(2,1)} collective-permute-done((bf16[1024,512]{1,0:T(8,128)(2,1)}, bf16[1024,512]{1,0:T(8,128)(2,1)}, u32[]{:S(2)}, u32[]{:S(2)}) %collective-permute-start.3) | collective-permute-done | bytes 1048608 | tf_op jit(solution)/shard_map/ppermute | solution.py:341
  54.9 3.8 %shard_map.120 = (bf16[1024,512]{1,0:T(8,128)(2,1)}, bf16[1024,512]{1,0:T(8,128)(2,1)}, f32[64,128]{1,0:T(8,128)}) custom-call(s32[2]{0:T(128)} %pad_add_fusion.me_ref, bf16[256,8192]{1,0:T(8,128)(2,1)} %x_ref.6, bf16[256,512]{1,0:T(8,128)(2,1)} %multiply_convert_fusion.1.c_ref, ...), custom_call_target="tpu_custom_call", output_to_operand_aliasing={{0}: (3, {}), {1}: (4, {}), {2}: (5, {})} | custom-call | bytes 4194304 | tf_op jit(solution)/shard_map/pallas_call | solution.py:139
  58.7 6.9 %collective-permute-start.6 = (f32[64,128]{1,0:T(8,128)}, f32[64,128]{1,0:T(8,128)S(1)}, u32[]{:S(2)}, u32[]{:S(2)}) collective-permute-start(f32[64,128]{1,0:T(8,128)} %get-tuple-element.44.refs_2_), channel_id=1, source_target_pairs={{0,8},{8,0},{1,9},{9,1},{2,10},{10,2},{3,11},{11,3},{4,12},{12,4},... | collective-permute-start | bytes 98312 | tf_op jit(solution)/shard_map/ppermute | solution.py:390
  66.9 4.1 %collective-permute-start.8 = (bf16[1024,512]{1,0:T(8,128)(2,1)}, bf16[1024,512]{1,0:T(8,128)(2,1)S(1)}, u32[]{:S(2)}, u32[]{:S(2)}) collective-permute-start(bf16[1024,512]{1,0:T(8,128)(2,1)} %get-tuple-element.45.refs_4_.refs_9_), channel_id=1, source_target_pairs={{1,0},{2,1},{3,2},{4,5},{5,6},{6,7},{9,8},{10,9},{11,10},{12,13},{... | collective-permute-start | bytes 3145736 | tf_op jit(solution)/shard_map/ppermute | solution.py:341
  70.9 15.0 %collective-permute-done.6.refs_5_ = f32[64,128]{1,0:T(8,128)S(1)} collective-permute-done((f32[64,128]{1,0:T(8,128)}, f32[64,128]{1,0:T(8,128)S(1)}, u32[]{:S(2)}, u32[]{:S(2)}) %collective-permute-start.6) | collective-permute-done | bytes 32800 | tf_op jit(solution)/shard_map/ppermute | solution.py:390
  87.0 3.8 %shard_map.121 = (bf16[1024,512]{1,0:T(8,128)(2,1)}, bf16[1024,512]{1,0:T(8,128)(2,1)}, f32[64,128]{1,0:T(8,128)}) custom-call(s32[2]{0:T(128)} %pad_add_fusion.me_ref, bf16[256,8192]{1,0:T(8,128)(2,1)} %x_ref.6, bf16[256,512]{1,0:T(8,128)(2,1)} %multiply_convert_fusion.1.c_ref, ...), custom_call_target="tpu_custom_call", output_to_operand_aliasing={{0}: (3, {}), {1}: (4, {}), {2}: (5, {})} | custom-call | flops 99999997952 | bytes 4194304 | tf_op jit(solution)/shard_map/pallas_call | solution.py:139
  92.1 5.0 %collective-permute-start.11 = (bf16[1024,512]{1,0:T(8,128)(2,1)}, bf16[1024,512]{1,0:T(8,128)(2,1)}, u32[]{:S(2)}, u32[]{:S(2)}) collective-permute-start(bf16[1024,512]{1,0:T(8,128)(2,1)} %get-tuple-element.48.refs_4_.refs_10_), channel_id=1, source_target_pairs={{1,0},{2,1},{3,2},{4,5},{5,6},{6,7},{9,8},{10,9},{11,10},{12,13},{... | collective-permute-start | bytes 3145736 | tf_op jit(solution)/shard_map/ppermute | solution.py:341
  102.2 3.8 %shard_map.122 = (bf16[1024,512]{1,0:T(8,128)(2,1)}, bf16[1024,512]{1,0:T(8,128)(2,1)}, f32[64,128]{1,0:T(8,128)}) custom-call(s32[2]{0:T(128)} %pad_add_fusion.me_ref, bf16[256,8192]{1,0:T(8,128)(2,1)} %x_ref.6, bf16[256,512]{1,0:T(8,128)(2,1)} %multiply_convert_fusion.1.c_ref, ...), custom_call_target="tpu_custom_call", output_to_operand_aliasing={{0}: (3, {}), {1}: (4, {}), {2}: (5, {})} | custom-call | bytes 4194304 | tf_op jit(solution)/shard_map/pallas_call | solution.py:139
  107.4 5.6 %collective-permute-start.12 = (bf16[1024,512]{1,0:T(8,128)(2,1)}, bf16[1024,512]{1,0:T(8,128)(2,1)}, u32[]{:S(2)}, u32[]{:S(2)}) collective-permute-start(bf16[1024,512]{1,0:T(8,128)(2,1)} %get-tuple-element.50.refs_3_.refs_11_), channel_id=1, source_target_pairs={{1,0},{2,1},{3,2},{4,5},{5,6},{6,7},{9,8},{10,9},{11,10},{12,13},{... | collective-permute-start | bytes 3145736 | tf_op jit(solution)/shard_map/ppermute | solution.py:341
  114.9 10.3 %all-to-all-start.1 = ((f32[32,64,128]{2,1,0:T(8,128)}), f32[32,64,128]{2,1,0:T(8,128)}, u32[]{:S(2)}, u32[]{:S(2)}) async-start(f32[32,64,128]{2,1,0:T(8,128)} %broadcast_in_dim.4), calls=%async_computation.1 | async-start | bytes 2097152 | tf_op jit(solution)/shard_map/all_to_all | solution.py:396
  126.1 2.9 %fusion.4.own_ref = f32[1024,512]{1,0:T(8,128)} fusion(bf16[256,512]{1,0:T(8,128)(2,1)S(1)} %copy-done.4, bf16[256,8192]{1,0:T(8,128)(2,1)} %x_ref.6, s32[]{:T(128)S(6)} %select_n.22), kind=kOutput, calls=%fused_computation.10 | convolution fusion | flops 268435456 | bytes 2883588 | tf_op jit(solution)/shard_map/dot_general | solution.py:22
  132.8 3.8 %shard_map.123 = (bf16[1024,512]{1,0:T(8,128)(2,1)}, bf16[1024,512]{1,0:T(8,128)(2,1)}) custom-call(s32[2]{0:T(128)} %pad_add_fusion.me_ref, bf16[256,8192]{1,0:T(8,128)(2,1)} %x_ref.6, bf16[256,512]{1,0:T(8,128)(2,1)} %multiply_convert_fusion.1.c_ref, bf16[1024,512]{1,0:T(8,128)(2,1)} %copy-done.8, ...), custom_call_target="tpu_custom_call" | custom-call | bytes 4194304 | tf_op jit(solution)/shard_map/pallas_call | solution.py:139
  137.8 6.9 %collective-permute-start.16 = (bf16[1024,512]{1,0:T(8,128)(2,1)}, bf16[1024,512]{1,0:T(8,128)(2,1)}, u32[]{:S(2)}, u32[]{:S(2)}) collective-permute-start(bf16[1024,512]{1,0:T(8,128)(2,1)} %get-tuple-element.52.refs_3_), channel_id=1, source_target_pairs={{1,0},{2,1},{3,2},{4,5},{5,6},{6,7},{9,8},{10,9},{11,10},{12,13},{... | collective-permute-start | bytes 3145736 | tf_op jit(solution)/shard_map/ppermute | solution.py:341
  146.2 3.8 %shard_map.124 = (bf16[1024,512]{1,0:T(8,128)(2,1)}, bf16[1024,512]{1,0:T(8,128)(2,1)}) custom-call(s32[2]{0:T(128)} %pad_add_fusion.me_ref, bf16[256,8192]{1,0:T(8,128)(2,1)} %x_ref.6, bf16[256,512]{1,0:T(8,128)(2,1)} %multiply_convert_fusion.1.c_ref, bf16[1024,512]{1,0:T(8,128)(2,1)} %collective-permute-done.10.refs_0_.refs_7_, ...), custom_call_target="tpu_custom_call" | custom-call | bytes 4194304 | tf_op jit(solution)/shard_map/pallas_call | solution.py:139
  151.3 6.8 %collective-permute-start.14 = (bf16[1024,512]{1,0:T(8,128)(2,1)}, bf16[1024,512]{1,0:T(8,128)(2,1)}, u32[]{:S(2)}, u32[]{:S(2)}) collective-permute-start(bf16[1024,512]{1,0:T(8,128)(2,1)} %get-tuple-element.54.refs_15_), channel_id=1, source_target_pairs={{1,0},{2,1},{3,2},{4,5},{5,6},{6,7},{9,8},{10,9},{11,10},{12,13},{... | collective-permute-start | bytes 3145736 | tf_op jit(solution)/shard_map/ppermute | solution.py:341
  158.1 13.0 %shard_map.125 = (bf16[256,512]{1,0:T(8,128)(2,1)}, bf16[256,8192]{1,0:T(8,128)(2,1)}) custom-call(s32[2]{0:T(128)} %pad_add_fusion.me_ref, bf16[256,8192]{1,0:T(8,128)(2,1)} %x_ref.6, bf16[256,512]{1,0:T(8,128)(2,1)} %c_ref.1, f32[256,1]{1,0:T(8,128)} %copy.26.inverse_ref, bf16[1024,512]{1,0:T(8,128)(2,1)} %shard_map.118.refs_0_, ...), custom_call_target="tpu_custom_call" | custom-call | flops 4294967296 | bytes 16777216 | tf_op jit(solution)/shard_map/pallas_call | solution.py:230
  178.1 8.9 %collective-permute-done.13.right_ref = bf16[1024,512]{1,0:T(8,128)(2,1)} collective-permute-done((bf16[1024,512]{1,0:T(8,128)(2,1)}, bf16[1024,512]{1,0:T(8,128)(2,1)}, u32[]{:S(2)}, u32[]{:S(2)}) %collective-permute-start.13) | collective-permute-done | bytes 1048608 | tf_op jit(solution)/shard_map/ppermute | solution.py:341
  187.0 3.4 %collective-permute-done.14.left_ref = bf16[1024,512]{1,0:T(8,128)(2,1)} collective-permute-done((bf16[1024,512]{1,0:T(8,128)(2,1)}, bf16[1024,512]{1,0:T(8,128)(2,1)}, u32[]{:S(2)}, u32[]{:S(2)}) %collective-permute-start.14) | collective-permute-done | bytes 1048608 | tf_op jit(solution)/shard_map/ppermute | solution.py:341
  (67 shorter events, 47.8 us)
Async XLA Ops:
  0.6 9.6 %copy-start.3 = (bf16[1,2048]{1,0:T(2,128)(2,1)S(1)}, bf16[1,2048]{1,0:T(2,128)(2,1)}, u32[]{:S(2)}) copy-start(bf16[1,2048]{1,0:T(2,128)(2,1)} %gain_ref.5) | copy-start | bytes 12292
  0.6 9.5 %copy-start = (bf16[1,2048,512]{2,1,0:T(8,128)(2,1)S(1)}, bf16[1,2048,512]{2,1,0:T(8,128)(2,1)}, u32[]{:S(2)}) copy-start(bf16[1,2048,512]{2,1,0:T(8,128)(2,1)} %param.9) | copy-start | bytes 6291460
  2.9 29.7 %collective-permute-start = (bf16[1024,512]{1,0:T(8,128)(2,1)}, bf16[1024,512]{1,0:T(8,128)(2,1)S(1)}, u32[]{:S(2)}, u32[]{:S(2)}) collective-permute-start(bf16[1024,512]{1,0:T(8,128)(2,1)} %shard_map.118.refs_0_), channel_id=1, source_target_pairs={{0,1},{1,2},{2,3},{5,4},{6,5},{7,6},{8,9},{9,10},{10,11},{13,12},{... | collective-permute-start | bytes 3145736 | tf_op jit(solution)/shard_map/ppermute | solution.py:341
  4.2 28.4 %collective-permute-start.1 = (bf16[1024,512]{1,0:T(8,128)(2,1)}, bf16[1024,512]{1,0:T(8,128)(2,1)}, u32[]{:S(2)}, u32[]{:S(2)}) collective-permute-start(bf16[1024,512]{1,0:T(8,128)(2,1)} %shard_map.118.refs_0_), channel_id=1, source_target_pairs={{1,0},{2,1},{3,2},{4,5},{5,6},{6,7},{9,8},{10,9},{11,10},{12,13},{... | collective-permute-start | bytes 3145736 | tf_op jit(solution)/shard_map/ppermute | solution.py:341
  11.5 37.4 %collective-permute-start.2 = (bf16[1024,512]{1,0:T(8,128)(2,1)}, bf16[1024,512]{1,0:T(8,128)(2,1)}, u32[]{:S(2)}, u32[]{:S(2)}) collective-permute-start(bf16[1024,512]{1,0:T(8,128)(2,1)} %multiply_convert_fusion.refs_1_), channel_id=1, source_target_pairs={{0,1},{1,2},{2,3},{5,4},{6,5},{7,6},{8,9},{9,10},{10,11},{13,12},{... | collective-permute-start | bytes 3145736 | tf_op jit(solution)/shard_map/ppermute | solution.py:341
  12.7 42.2 %collective-permute-start.3 = (bf16[1024,512]{1,0:T(8,128)(2,1)}, bf16[1024,512]{1,0:T(8,128)(2,1)}, u32[]{:S(2)}, u32[]{:S(2)}) collective-permute-start(bf16[1024,512]{1,0:T(8,128)(2,1)} %multiply_convert_fusion.refs_1_), channel_id=1, source_target_pairs={{1,0},{2,1},{3,2},{4,5},{5,6},{6,7},{9,8},{10,9},{11,10},{12,13},{... | collective-permute-start | bytes 3145736 | tf_op jit(solution)/shard_map/ppermute | solution.py:341
  20.8 24.2 %all-to-all-start = ((f32[32,64,128]{2,1,0:T(8,128)}), f32[32,64,128]{2,1,0:T(8,128)}, u32[]{:S(2)}, u32[]{:S(2)}) async-start(f32[32,64,128]{2,1,0:T(8,128)} %bitcast.26), calls=%async_computation | async-start | bytes 2097152 | tf_op jit(solution)/shard_map/all_to_all | solution.py:369
  28.0 3.2 %copy-start.11 = (bf16[256,512]{1,0:T(8,128)(2,1)S(1)}, bf16[256,512]{1,0:T(8,128)(2,1)}, u32[]{:S(2)}) copy-start(bf16[256,512]{1,0:T(8,128)(2,1)} %c_ref.1) | copy-start | bytes 786436
  37.4 48.6 %collective-permute-start.4 = (bf16[1024,512]{1,0:T(8,128)(2,1)}, bf16[1024,512]{1,0:T(8,128)(2,1)S(1)}, u32[]{:S(2)}, u32[]{:S(2)}) collective-permute-start(bf16[1024,512]{1,0:T(8,128)(2,1)} %get-tuple-element.40.refs_3_.refs_2_), channel_id=1, source_target_pairs={{0,1},{1,2},{2,3},{5,4},{6,5},{7,6},{8,9},{9,10},{10,11},{13,12},{... | collective-permute-start | bytes 3145736 | tf_op jit(solution)/shard_map/ppermute | solution.py:341
  38.7 47.3 %collective-permute-start.5 = (bf16[1024,512]{1,0:T(8,128)(2,1)}, bf16[1024,512]{1,0:T(8,128)(2,1)}, u32[]{:S(2)}, u32[]{:S(2)}) collective-permute-start(bf16[1024,512]{1,0:T(8,128)(2,1)} %get-tuple-element.42.refs_4_.refs_8_), channel_id=1, source_target_pairs={{1,0},{2,1},{3,2},{4,5},{5,6},{6,7},{9,8},{10,9},{11,10},{12,13},{... | collective-permute-start | bytes 3145736 | tf_op jit(solution)/shard_map/ppermute | solution.py:341
  58.7 27.3 %collective-permute-start.6 = (f32[64,128]{1,0:T(8,128)}, f32[64,128]{1,0:T(8,128)S(1)}, u32[]{:S(2)}, u32[]{:S(2)}) collective-permute-start(f32[64,128]{1,0:T(8,128)} %get-tuple-element.44.refs_2_), channel_id=1, source_target_pairs={{0,8},{8,0},{1,9},{9,1},{2,10},{10,2},{3,11},{11,3},{4,12},{12,4},... | collective-permute-start | bytes 98312 | tf_op jit(solution)/shard_map/ppermute | solution.py:390
  65.6 32.8 %collective-permute-start.7 = (bf16[1024,512]{1,0:T(8,128)(2,1)}, bf16[1024,512]{1,0:T(8,128)(2,1)S(1)}, u32[]{:S(2)}, u32[]{:S(2)}) collective-permute-start(bf16[1024,512]{1,0:T(8,128)(2,1)} %get-tuple-element.43.refs_3_), channel_id=1, source_target_pairs={{0,1},{1,2},{2,3},{5,4},{6,5},{7,6},{8,9},{9,10},{10,11},{13,12},{... | collective-permute-start | bytes 3145736 | tf_op jit(solution)/shard_map/ppermute | solution.py:341
  66.9 34.4 %collective-permute-start.8 = (bf16[1024,512]{1,0:T(8,128)(2,1)}, bf16[1024,512]{1,0:T(8,128)(2,1)S(1)}, u32[]{:S(2)}, u32[]{:S(2)}) collective-permute-start(bf16[1024,512]{1,0:T(8,128)(2,1)} %get-tuple-element.45.refs_4_.refs_9_), channel_id=1, source_target_pairs={{1,0},{2,1},{3,2},{4,5},{5,6},{6,7},{9,8},{10,9},{11,10},{12,13},{... | collective-permute-start | bytes 3145736 | tf_op jit(solution)/shard_map/ppermute | solution.py:341
  90.8 41.0 %collective-permute-start.9 = (bf16[1024,512]{1,0:T(8,128)(2,1)}, bf16[1024,512]{1,0:T(8,128)(2,1)S(1)}, u32[]{:S(2)}, u32[]{:S(2)}) collective-permute-start(bf16[1024,512]{1,0:T(8,128)(2,1)} %get-tuple-element.46.refs_3_.refs_4_), channel_id=1, source_target_pairs={{0,1},{1,2},{2,3},{5,4},{6,5},{7,6},{8,9},{9,10},{10,11},{13,12},{... | collective-permute-start | bytes 3145736 | tf_op jit(solution)/shard_map/ppermute | solution.py:341
  92.1 39.7 %collective-permute-start.11 = (bf16[1024,512]{1,0:T(8,128)(2,1)}, bf16[1024,512]{1,0:T(8,128)(2,1)}, u32[]{:S(2)}, u32[]{:S(2)}) collective-permute-start(bf16[1024,512]{1,0:T(8,128)(2,1)} %get-tuple-element.48.refs_4_.refs_10_), channel_id=1, source_target_pairs={{1,0},{2,1},{3,2},{4,5},{5,6},{6,7},{9,8},{10,9},{11,10},{12,13},{... | collective-permute-start | bytes 3145736 | tf_op jit(solution)/shard_map/ppermute | solution.py:341
  106.0 20.1 %copy-start.4 = (bf16[256,512]{1,0:T(8,128)(2,1)S(1)}, bf16[256,512]{1,0:T(8,128)(2,1)}, u32[]{:S(2)}) copy-start(bf16[256,512]{1,0:T(8,128)(2,1)} %multiply_convert_fusion.1.c_ref) | copy-start | bytes 786436
  106.0 38.8 %collective-permute-start.10 = (bf16[1024,512]{1,0:T(8,128)(2,1)}, bf16[1024,512]{1,0:T(8,128)(2,1)}, u32[]{:S(2)}, u32[]{:S(2)}) collective-permute-start(bf16[1024,512]{1,0:T(8,128)(2,1)} %get-tuple-element.49.refs_2_.refs_5_), channel_id=1, source_target_pairs={{0,1},{1,2},{2,3},{5,4},{6,5},{7,6},{8,9},{9,10},{10,11},{13,12},{... | collective-permute-start | bytes 3145736 | tf_op jit(solution)/shard_map/ppermute | solution.py:341
  107.4 38.8 %collective-permute-start.12 = (bf16[1024,512]{1,0:T(8,128)(2,1)}, bf16[1024,512]{1,0:T(8,128)(2,1)}, u32[]{:S(2)}, u32[]{:S(2)}) collective-permute-start(bf16[1024,512]{1,0:T(8,128)(2,1)} %get-tuple-element.50.refs_3_.refs_11_), channel_id=1, source_target_pairs={{1,0},{2,1},{3,2},{4,5},{5,6},{6,7},{9,8},{10,9},{11,10},{12,13},{... | collective-permute-start | bytes 3145736 | tf_op jit(solution)/shard_map/ppermute | solution.py:341
  114.9 56.2 %all-to-all-start.1 = ((f32[32,64,128]{2,1,0:T(8,128)}), f32[32,64,128]{2,1,0:T(8,128)}, u32[]{:S(2)}, u32[]{:S(2)}) async-start(f32[32,64,128]{2,1,0:T(8,128)} %broadcast_in_dim.4), calls=%async_computation.1 | async-start | bytes 2097152 | tf_op jit(solution)/shard_map/all_to_all | solution.py:396
  136.5 38.0 %collective-permute-start.15 = (bf16[1024,512]{1,0:T(8,128)(2,1)}, bf16[1024,512]{1,0:T(8,128)(2,1)S(1)}, u32[]{:S(2)}, u32[]{:S(2)}) collective-permute-start(bf16[1024,512]{1,0:T(8,128)(2,1)} %get-tuple-element.51.refs_2_), channel_id=1, source_target_pairs={{0,1},{1,2},{2,3},{5,4},{6,5},{7,6},{8,9},{9,10},{10,11},{13,12},{... | collective-permute-start | bytes 3145736 | tf_op jit(solution)/shard_map/ppermute | solution.py:341
  137.8 36.7 %collective-permute-start.16 = (bf16[1024,512]{1,0:T(8,128)(2,1)}, bf16[1024,512]{1,0:T(8,128)(2,1)}, u32[]{:S(2)}, u32[]{:S(2)}) collective-permute-start(bf16[1024,512]{1,0:T(8,128)(2,1)} %get-tuple-element.52.refs_3_), channel_id=1, source_target_pairs={{1,0},{2,1},{3,2},{4,5},{5,6},{6,7},{9,8},{10,9},{11,10},{12,13},{... | collective-permute-start | bytes 3145736 | tf_op jit(solution)/shard_map/ppermute | solution.py:341
  150.0 37.0 %collective-permute-start.13 = (bf16[1024,512]{1,0:T(8,128)(2,1)}, bf16[1024,512]{1,0:T(8,128)(2,1)}, u32[]{:S(2)}, u32[]{:S(2)}) collective-permute-start(bf16[1024,512]{1,0:T(8,128)(2,1)} %get-tuple-element.53.refs_14_), channel_id=1, source_target_pairs={{0,1},{1,2},{2,3},{5,4},{6,5},{7,6},{8,9},{9,10},{10,11},{13,12},{... | collective-permute-start | bytes 3145736 | tf_op jit(solution)/shard_map/ppermute | solution.py:341
  151.3 39.1 %collective-permute-start.14 = (bf16[1024,512]{1,0:T(8,128)(2,1)}, bf16[1024,512]{1,0:T(8,128)(2,1)}, u32[]{:S(2)}, u32[]{:S(2)}) collective-permute-start(bf16[1024,512]{1,0:T(8,128)(2,1)} %get-tuple-element.54.refs_15_), channel_id=1, source_target_pairs={{1,0},{2,1},{3,2},{4,5},{5,6},{6,7},{9,8},{10,9},{11,10},{12,13},{... | collective-permute-start | bytes 3145736 | tf_op jit(solution)/shard_map/ppermute | solution.py:341
  174.6 15.8 %copy-start.2 = (f32[1024,512]{1,0:T(8,128)S(1)}, f32[1024,512]{1,0:T(8,128)}, u32[]{:S(2)}) copy-start(f32[1024,512]{1,0:T(8,128)} %fusion.4.own_ref) | copy-start | bytes 6291460
  (9 other events, 13.1 us)
